TPU v7x, 32 devices: a whole 2x2x4 slice. The times are simulated.
32 devices in a mesh: seq: 16 (over z, x, core), tp: 2 (over y).
Axes of the slice: x: 2, y: 2, z: 4, core: 2. Of those that a mesh axis runs over, the one named last changes fastest.
Arguments:
- residual: bfloat16 [4096, 5376], P('seq', 'tp'), may hold values from -10.5 to 10.5
- input_gain: float32 [5376], replicated, may hold values from 0.25 to 1.75
- w_query: bfloat16 [5376, 4096], P('seq', 'tp'), may hold values from -0.078125 to 0.078125
- key_weight: bfloat16 [5376, 2048], P('seq', 'tp'), may hold values from -0.078125 to 0.078125
- value_weight: bfloat16 [5376, 2048], P('seq', 'tp'), may hold values from -0.078125 to 0.078125
- query_gain: float32 [128], replicated, may hold values from 0.25 to 1.75
- key_gain: float32 [128], replicated, may hold values from 0.25 to 1.75
- w_out: bfloat16 [4096, 5376], P('tp', 'seq'), may hold values from -0.1640625 to 0.1640625
- post_gain: float32 [5376], replicated, may hold values from 0.25 to 1.75
- positions: int32 [4096], replicated, may hold values from 0 to 5631, as said below
Outputs:
- mixed: bfloat16 [4096, 5376], P('seq', 'tp')
Inputs may be any that keep to these rules, and one draw needn't show every extreme that they name: positions start at 0 and rise by 1 over the first 1024 tokens; after that they rise by 1 or 2 from each token to the next, by 2 at exactly (3072) // 2 tokens.
All inputs are finite; a program needn't handle non-finite values.
Results may differ from a plain program's by a relative error of at most 0.017.
Values may be sent and summed in bfloat16 or wider, within the bound.
A program may use at most 128 MiB of HBM per device.

v0:
```python
import jax
import jax.numpy as jnp
from jax import lax
from jax.sharding import PartitionSpec as P

LOOKBACK_SPAN = 1024


epsilon = 1e-06
score_scale = 168.0 ** (-0.5)
rotary_base = 10000.0


def from_behind(block, axis, distance):
    devices = range(lax.axis_size(axis))
    route = [(i - distance, i) for i in devices if i - distance in devices]
    return lax.ppermute(block, axis, route)


def norm_scale(value_matrix, gain):
    mean_square = jnp.mean(value_matrix * value_matrix, axis=-1, keepdims=True)
    return value_matrix * lax.rsqrt(mean_square + epsilon) * gain


def rotary(value_matrix, places):
    half_dim = value_matrix.shape[-1] // 2
    inverse = rotary_base ** (-jnp.arange(half_dim, dtype=jnp.float32) / half_dim)
    angles = places.astype(jnp.float32)[:, None] * inverse[None, :]
    cosine = jnp.cos(angles)[:, None, :]
    sine = jnp.sin(angles)[:, None, :]
    first = value_matrix[..., :half_dim]
    second = value_matrix[..., half_dim:]
    return jnp.concatenate(
        [first * cosine - second * sine, second * cosine + first * sine], axis=-1
    )


def local(
    residual,
    input_gain,
    w_query,
    key_weight,
    value_weight,
    query_gain,
    key_gain,
    w_out,
    post_gain,
    positions,
):
    tok_rows = residual.shape[0]
    seq_at = lax.axis_index("seq")
    tp_at = lax.axis_index("tp")
    head_dim = query_gain.shape[0]
    local_kv = key_weight.shape[1] // head_dim
    query_group = w_query.shape[1] // key_weight.shape[1]
    gathered = lax.all_gather(residual, "tp", axis=1, tiled=True)
    normalized_input = norm_scale(gathered.astype(jnp.float32), input_gain).astype(jnp.bfloat16)
    own_places = lax.dynamic_slice_in_dim(positions, seq_at * tok_rows, tok_rows, 0)
    reach = (LOOKBACK_SPAN - 2) // tok_rows + 1

    def attend(query_matrix, stacked, key_places, valid):
        key_matrix = stacked[0].reshape(-1, local_kv, head_dim)
        value_matrix = stacked[1].reshape(-1, local_kv, head_dim)
        scores = (
            jnp.einsum(
                "qkgd,skd->kgqs", query_matrix, key_matrix, preferred_element_type=jnp.float32
            )
            * score_scale
        )
        distance = own_places[:, None] - key_places[None, :]
        allowed = valid[None, :] & (distance >= 0) & (distance < LOOKBACK_SPAN)
        weights = jnp.where(allowed[None, None], jnp.exp(scores), jnp.zeros_like(scores))
        total = jnp.sum(weights, axis=-1)
        summed = jnp.einsum(
            "kgqs,skd->qkgd",
            weights.astype(jnp.bfloat16),
            value_matrix,
            preferred_element_type=jnp.float32,
        )
        return (total, summed)

    pieces = (
        lax.all_gather(w_query, "seq", axis=0, tiled=True),
        lax.all_gather(key_weight, "seq", axis=0, tiled=True),
        lax.all_gather(value_weight, "seq", axis=0, tiled=True),
    )
    queries_raw, unrotated_keys, projected_values = tuple(
        (jnp.dot(normalized_input, piece, preferred_element_type=jnp.float32) for piece in pieces)
    )
    key_matrix = rotary(
        norm_scale(unrotated_keys.reshape(tok_rows, local_kv, head_dim), key_gain), own_places
    )
    stacked = jnp.stack(
        [key_matrix.reshape(tok_rows, local_kv * head_dim), projected_values]
    ).astype(jnp.bfloat16)
    pieces = []
    for distance in range(reach, 0, -1):
        pieces.append(from_behind(stacked, "seq", distance))
    halo = jnp.concatenate(pieces, axis=1)
    query_matrix = rotary(
        norm_scale(queries_raw.reshape(tok_rows, local_kv * query_group, head_dim), query_gain),
        own_places,
    )
    query_matrix = query_matrix.astype(jnp.bfloat16).reshape(
        tok_rows, local_kv, query_group, head_dim
    )
    inner_total, inner_sum = attend(
        query_matrix, stacked, own_places, jnp.ones((tok_rows,), jnp.bool_)
    )
    span = halo.shape[1]
    padded_places = jnp.concatenate([jnp.zeros((span,), jnp.int32), positions])
    halo_places = lax.dynamic_slice_in_dim(padded_places, seq_at * tok_rows, span, 0)
    halo_valid = seq_at * tok_rows - span + jnp.arange(span, dtype=jnp.int32) >= 0
    outer_total, outer_sum = attend(query_matrix, halo, halo_places, halo_valid)
    total = jnp.transpose(inner_total + outer_total, (2, 0, 1))
    merged = (inner_sum + outer_sum) / total[..., None]
    attended = merged.astype(jnp.bfloat16).reshape(tok_rows, local_kv * query_group * head_dim)
    partial_out = jnp.dot(
        attended,
        lax.all_gather(w_out, "seq", axis=1, tiled=True),
        preferred_element_type=jnp.float32,
    )
    summed_cols = lax.psum_scatter(
        partial_out.astype(jnp.bfloat16), "tp", scatter_dimension=1, tiled=True
    ).astype(jnp.float32)
    full_width = post_gain.shape[0]
    squares = lax.psum(jnp.sum(summed_cols * summed_cols, axis=1), "tp")
    inverse_rms = lax.rsqrt(squares / full_width + epsilon)
    gain_part = lax.dynamic_slice_in_dim(
        post_gain, tp_at * summed_cols.shape[1], summed_cols.shape[1], 0
    )
    return (residual.astype(jnp.float32) + summed_cols * inverse_rms[:, None] * gain_part).astype(
        jnp.bfloat16
    )


def solution(mesh):
    in_specs = (
        P("seq", "tp"),
        P(),
        P("seq", "tp"),
        P("seq", "tp"),
        P("seq", "tp"),
        P(),
        P(),
        P("tp", "seq"),
        P(),
        P(),
    )
    out_specs = P("seq", "tp")
    return jax.shard_map(local, mesh=mesh, in_specs=in_specs, out_specs=out_specs, check_vma=False)
```

profile of v0, /device:TPU:0, one launch (start us, length us, event | category | flops | bytes accessed | tf_op | source)
XLA Modules:
  0.0 613.0 jit_solution(4301716352663828676)
XLA Ops:
  11.1 41.0 %all-gather.6.cloned.1.call-done = bf16[256,5376]{1,0:T(8,128)(2,1)} async-done(((bf16[256,2688]{1,0:T(8,128)(2,1)}), bf16[256,5376]{1,0:T(8,128)(2,1)}) %all-gather.6.cloned.1.call-update) | async-done | bytes 2752528 | tf_op jit(solution)/shard_map/all_gather | solution.py:56
  52.1 2.4 fusion.7
  54.6 91.0 %all-gather.10.cloned.1.call-done = bf16[5376,1024]{1,0:T(8,128)(2,1)} async-done(((bf16[336,1024]{1,0:T(8,128)(2,1)}), bf16[5376,1024]{1,0:T(8,128)(2,1)}) %all-gather.10.cloned.1.call-update) | async-done | bytes 11010064 | tf_op jit(solution)/shard_map/all_gather | solution.py:84
  145.6 6.7 %fusion.39 = f32[256,1024]{1,0:T(8,128)S(1)} fusion(bf16[5376,1024]{1,0:T(8,128)(2,1)} %all-gather.10.cloned.1.call-done, bf16[256,5376]{1,0:T(8,128)(2,1)} %all-gather.6.cloned.1.call-done, f32[5376]{0:T(1024)S(1)} %copy-done.13, f32[256]{0:T(256)S(1)} %add_rsqrt_fusion.3), kind=kOutput, calls=%fused_computation.74 | convolution fusion | flops 2824077312 | bytes 14833664 | tf_op jit(solution)/shard_map/dot_general | solution.py:88
  155.2 2.1 stack_reshape.4
  157.3 79.9 %all-gather.8.cloned.1.call-done = bf16[5376,1024]{1,0:T(8,128)(2,1)} async-done(((bf16[336,1024]{1,0:T(8,128)(2,1)}), bf16[5376,1024]{1,0:T(8,128)(2,1)}) %all-gather.8.cloned.1.call-update) | async-done | bytes 11010064 | tf_op jit(solution)/shard_map/all_gather | solution.py:85
  237.2 7.2 %convolution_convert_fusion.1 = bf16[256,1024]{1,0:T(8,128)(2,1)S(1)} fusion(bf16[5376,1024]{1,0:T(8,128)(2,1)} %all-gather.8.cloned.1.call-done, bf16[256,5376]{1,0:T(8,128)(2,1)S(1)} %copy-done.1, f32[5376]{0:T(1024)} %param.11, f32[256]{0:T(256)} %copy-done.10), kind=kOutput, calls=%fused_computation.38 | convolution fusion | flops 2824339456 | bytes 14309376 | tf_op jit(solution)/shard_map/dot_general | solution.py:88
  245.4 3.3 collective-permute-start
  248.6 3.0 collective-permute-start.1
  251.6 3.6 collective-permute-start.2
  255.2 2.3 collective-permute-start.3
  257.6 1.4 fusion.31
  259.1 2.0 fusion.28
  262.3 31.3 %collective-permute-done = bf16[2,256,1024]{2,1,0:T(8,128)(2,1)} collective-permute-done((bf16[2,256,1024]{2,1,0:T(8,128)(2,1)S(1)}, bf16[2,256,1024]{2,1,0:T(8,128)(2,1)}, u32[]{:S(2)}, u32[]{:S(2)}) %collective-permute-start) | collective-permute-done | bytes 1048608 | tf_op jit(solution)/shard_map/ppermute | solution.py:17
  293.6 1.3 constant_dynamic-update-slice_fusion.3
  297.2 43.6 %collective-permute-done.2 = bf16[2,256,1024]{2,1,0:T(8,128)(2,1)S(1)} collective-permute-done((bf16[2,256,1024]{2,1,0:T(8,128)(2,1)S(1)}, bf16[2,256,1024]{2,1,0:T(8,128)(2,1)S(1)}, u32[]{:S(2)}, u32[]{:S(2)}) %collective-permute-start.2) | collective-permute-done | bytes 1048608 | tf_op jit(solution)/shard_map/ppermute | solution.py:17
  342.2 2.0 slice_bitcast_fusion
  344.2 4.0 copy.60
  348.2 2.0 copy.68
  350.2 50.0 %all-gather.12.cloned.1.call-done = bf16[5376,2048]{1,0:T(8,128)(2,1)} async-done(((bf16[336,2048]{1,0:T(8,128)(2,1)}), bf16[5376,2048]{1,0:T(8,128)(2,1)}) %all-gather.12.cloned.1.call-update) | async-done | bytes 22020112 | tf_op jit(solution)/shard_map/all_gather | solution.py:83
  400.2 11.1 %convolution_bitcast_fusion = f32[32,8,16,128]{3,1,2,0:T(8,128)S(1)} fusion(bf16[5376,2048]{1,0:T(8,128)(2,1)} %all-gather.12.cloned.1.call-done, bf16[256,5376]{1,0:T(8,128)(2,1)} %all-gather.6.cloned.1.call-done, f32[5376]{0:T(1024)S(1)} %copy-done.14, f32[256]{0:T(256)S(1)} %copy-done.11), kind=kOutput, calls=%fused_computation.35 | convolution fusion | flops 5642649600 | bytes 26892288 | tf_op jit(solution)/shard_map/dot_general | solution.py:88
  413.8 1.4 multiply_multiply_fusion
  416.9 1.5 fusion.10
  418.5 8.1 %fusion = (f32[8,2,256]{2,1,0:T(2,128)S(1)}, f32[8,1024,256,2]{2,1,3,0:T(8,128)}) fusion(pred[256,1024]{0,1:T(8,128)(4,1)S(1)} %copy-done.7, bf16[256,8,2,64]{3,0,2,1:T(8,128)(2,1)S(1)} %bitcast.81, bf16[256,8,2,64]{3,0,2,1:T(8,128)(2,1)S(1)} %bitcast.83, bf16[1024,8,128,1]{2,1,0,3:T(8,128)(2,1)S(1)} %bitcast.76), kind=kOutput, calls=%fused_computation.1 | convolution fusion | flops 1088417792 | bytes 20201472 | tf_op jit(solution)/shard_map/qkgd,skd->kgqs/dot_general | solution.py:65
  428.2 10.2 %fusion.18 = bf16[256,8,2,128]{0,3,2,1:T(8,128)(2,1)} fusion(f32[8,128,2,256]{3,1,2,0:T(8,128)S(1)} %fusion.16, bf16[1024,8,128,1]{0,2,3,1:T(8,128)(2,1)S(1)} %bitcast.75, f32[8,1024,256,2]{2,1,3,0:T(8,128)} %get-tuple-element.18, pred[256,1024]{0,1:T(8,128)(4,1)S(1)} %copy-done.7, f32[256,8,2]{0,2,1:T(2,128)S(1)} %add_bitcast_fusion), kind=kOutput, calls=%fused_computation.25 | convolution fusion | flops 1087897600 | bytes 22298624 | tf_op jit(solution)/shard_map/kgqs,skd->qkgd/dot_general | solution.py:74
  438.4 106.1 %all-gather.14.cloned.1.call-done = bf16[2048,5376]{0,1:T(8,128)(2,1)} async-done(((bf16[2048,336]{0,1:T(8,128)(2,1)}), bf16[2048,5376]{0,1:T(8,128)(2,1)}) %all-gather.14.cloned.1.call-update) | async-done | bytes 22020112 | tf_op jit(solution)/shard_map/all_gather | solution.py:120
  544.5 10.9 %convolution_convert_fusion = bf16[256,5376]{1,0:T(8,128)(2,1)S(1)} fusion(bf16[256,2048]{0,1:T(8,128)(2,1)} %bitcast.84, bf16[2048,5376]{0,1:T(8,128)(2,1)} %all-gather.14.cloned.1.call-done), kind=kOutput, calls=%fused_computation.7 | convolution fusion | flops 5638520832 | bytes 25821184 | tf_op jit(solution)/shard_map/dot_general | solution.py:118
  555.4 2.8 copy.63
  558.9 38.4 %reduce-scatter.4.cloned.1.call-done = bf16[2688,256]{1,0:T(8,128)(2,1)} async-done(((bf16[5376,256]{1,0:T(8,128)(2,1)}), bf16[2688,256]{1,0:T(8,128)(2,1)}) %reduce-scatter.4.cloned.1.call-update) | async-done | bytes 1376272
  597.3 1.8 copy.64
  599.5 4.9 psum.7
  604.4 1.7 fusion.15
  (76 shorter events, 20.0 us)
Async XLA Ops:
  6.5 3.5 copy-start.8
  6.5 45.6 %all-gather.6.cloned.1.call-start = ((), (), s32[]{:S(2)}) async-start(), calls=%async_computation.1 | async-start | bytes 4128768 | tf_op jit(solution)/shard_map/all_gather | solution.py:56
  7.3 138.3 %all-gather.10.cloned.1.call-start = ((), (), s32[]{:S(2)}) async-start(), calls=%async_computation.3 | async-start | bytes 11698176 | tf_op jit(solution)/shard_map/all_gather | solution.py:84
  8.0 229.2 %all-gather.8.cloned.1.call-start = ((), (), s32[]{:S(2)}) async-start(), calls=%async_computation.2 | async-start | bytes 11698176 | tf_op jit(solution)/shard_map/all_gather | solution.py:85
  8.7 136.8 %copy-start.13 = (f32[5376]{0:T(1024)S(1)}, f32[5376]{0:T(1024)}, u32[]{:S(2)}) copy-start(f32[5376]{0:T(1024)} %param.11) | copy-start | bytes 64516
  8.8 391.4 %all-gather.12.cloned.1.call-start = ((), (), s32[]{:S(2)}) async-start(), calls=%async_computation.4 | async-start | bytes 23396352 | tf_op jit(solution)/shard_map/all_gather | solution.py:83
  9.3 535.2 %all-gather.14.cloned.1.call-start = ((), (), s32[]{:S(2)}) async-start(), calls=%async_computation.5 | async-start | bytes 23396352 | tf_op jit(solution)/shard_map/all_gather | solution.py:120
  9.9 587.4 %reduce-scatter.4.cloned.1.call-start = ((), (), s32[]{:S(2)}) async-start(), calls=%async_computation.6 | async-start | bytes 4128768
  54.6 97.7 %copy-start.10 = (f32[256]{0:T(256)}, f32[256]{0:T(256)S(1)}, u32[]{:S(2)}) copy-start(f32[256]{0:T(256)S(1)} %add_rsqrt_fusion.3) | copy-start | bytes 3076
  152.3 0.7 copy-start.12
  153.3 83.9 %copy-start.1 = (bf16[256,5376]{1,0:T(8,128)(2,1)S(1)}, bf16[256,5376]{1,0:T(8,128)(2,1)}, u32[]{:S(2)}) copy-start(bf16[256,5376]{1,0:T(8,128)(2,1)} %all-gather.6.cloned.1.call-done) | copy-start | bytes 8257540
  237.2 8.1 %copy-start.5 = (bf16[1,256,1024]{2,1,0:T(8,128)(2,1)S(1)}, bf16[1,256,1024]{2,1,0:T(8,128)(2,1)}, u32[]{:S(2)}) copy-start(bf16[1,256,1024]{2,1,0:T(8,128)(2,1)} %stack_reshape.4) | copy-start | bytes 1572868
  244.5 0.8 copy-start.4
  245.4 48.3 %collective-permute-start = (bf16[2,256,1024]{2,1,0:T(8,128)(2,1)S(1)}, bf16[2,256,1024]{2,1,0:T(8,128)(2,1)}, u32[]{:S(2)}, u32[]{:S(2)}) collective-permute-start(bf16[2,256,1024]{2,1,0:T(8,128)(2,1)S(1)} %pad_maximum_fusion.1), channel_id=1, source_target_pairs={{0,8},{2,10},{4,12},{6,14},{8,16},{10,18},{12,20},{14,22},{16,24},... | collective-permute-start | bytes 3145736 | tf_op jit(solution)/shard_map/ppermute | solution.py:17
  248.6 47.2 %collective-permute-start.1 = (bf16[2,256,1024]{2,1,0:T(8,128)(2,1)S(1)}, bf16[2,256,1024]{2,1,0:T(8,128)(2,1)}, u32[]{:S(2)}, u32[]{:S(2)}) collective-permute-start(bf16[2,256,1024]{2,1,0:T(8,128)(2,1)S(1)} %pad_maximum_fusion.1), channel_id=1, source_target_pairs={{0,6},{2,8},{4,10},{6,12},{8,14},{10,16},{12,18},{14,20},{16,22},{... | collective-permute-start | bytes 3145736 | tf_op jit(solution)/shard_map/ppermute | solution.py:17
  251.6 89.2 %collective-permute-start.2 = (bf16[2,256,1024]{2,1,0:T(8,128)(2,1)S(1)}, bf16[2,256,1024]{2,1,0:T(8,128)(2,1)S(1)}, u32[]{:S(2)}, u32[]{:S(2)}) collective-permute-start(bf16[2,256,1024]{2,1,0:T(8,128)(2,1)S(1)} %pad_maximum_fusion.1), channel_id=1, source_target_pairs={{0,4},{2,6},{4,8},{6,10},{8,12},{10,14},{12,16},{14,18},{16,20},{1... | collective-permute-start | bytes 3145736 | tf_op jit(solution)/shard_map/ppermute | solution.py:17
  255.2 85.7 %collective-permute-start.3 = (bf16[2,256,1024]{2,1,0:T(8,128)(2,1)S(1)}, bf16[2,256,1024]{2,1,0:T(8,128)(2,1)}, u32[]{:S(2)}, u32[]{:S(2)}) collective-permute-start(bf16[2,256,1024]{2,1,0:T(8,128)(2,1)S(1)} %pad_maximum_fusion.1), channel_id=1, source_target_pairs={{0,2},{2,4},{4,6},{6,8},{8,10},{10,12},{12,14},{14,16},{16,18},{18... | collective-permute-start | bytes 3145736 | tf_op jit(solution)/shard_map/ppermute | solution.py:17
  348.2 52.0 %copy-start.11 = (f32[256]{0:T(256)S(1)}, f32[256]{0:T(256)}, u32[]{:S(2)}) copy-start(f32[256]{0:T(256)} %copy-done.10) | copy-start | bytes 3076
  348.2 52.0 %copy-start.14 = (f32[5376]{0:T(1024)S(1)}, f32[5376]{0:T(1024)}, u32[]{:S(2)}) copy-start(f32[5376]{0:T(1024)} %param.11) | copy-start | bytes 64516
  416.0 0.8 copy-start.6
  416.9 1.6 copy-start.3
  416.9 1.6 copy-start.7
  426.6 1.6 copy-start.2
  558.1 0.7 copy-start.9
  558.2 46.3 %copy-start = (bf16[256,2688]{1,0:T(8,128)(2,1)S(1)}, bf16[256,2688]{1,0:T(8,128)(2,1)}, u32[]{:S(2)}) copy-start(bf16[256,2688]{1,0:T(8,128)(2,1)} %param.10) | copy-start | bytes 4128772
Sparse Core Ops, SparseCore 0:
  8.9 43.1 all-gather.5
  54.4 91.0 all-gather.9
  147.8 89.3 all-gather.7
  238.6 161.4 all-gather.11
  401.6 142.8 all-gather.13
  558.3 39.0 reduce-scatter.3
where the time goes:
time: 614 us; the launch traced here: 613 us
  waiting for transfers between devices  485 us (79%)
  matrix products  56.6 us (9%)
  local copies, waits for them, and re-layouts  25.8 us (4%)
  other arithmetic  14.1 us (2%)
  between operations  13.8 us (2%)
  starting transfers between devices  12.4 us (2%)
    all_gather x1, waiting for transfers between devices, local(): lax.all_gather(w_out, 'seq', axis=1, tiled=True)  106 us
    all_gather x1, waiting for transfers between devices, local(): lax.all_gather(key_weight, 'seq', axis=0, tiled=True)  91 us
    all_gather x1, waiting for transfers between devices, local(): lax.all_gather(value_weight, 'seq', axis=0, tiled=True)  79.9 us
    ppermute x4, waiting for transfers between devices, from_behind(): return lax.ppermute(block, axis, route)  75.9 us
    all_gather x1, waiting for transfers between devices, local(): lax.all_gather(w_query, 'seq', axis=0, tiled=True)  50 us
    unnamed x7, waiting for transfers between devices  41.5 us
    all_gather x1, waiting for transfers between devices, local(): gathered = lax.all_gather(residual, 'tp', axis=1, tiled=True)  41 us
    dot_general x3, matrix products, local(): jnp.dot(normalized_input, piece, preferred_element_type=jnp.float32)  25.1 us
  transfers between devices with their start and end apart: 10, of which 9 were waited for; matrix products, arithmetic and copies ran while one was open for 12% of the time, Pallas kernels for 0%

commit v1 on v0

--- a/solution.py
+++ b/solution.py
@@ -1,6 +1,7 @@
 import jax
 import jax.numpy as jnp
 from jax import lax
+from jax.sharding import Mesh
 from jax.sharding import PartitionSpec as P
 
 LOOKBACK_SPAN = 1024
@@ -134,18 +135,195 @@
     )
 
 
+def swap(block, axis):
+    size = lax.axis_size(axis)
+    return lax.ppermute(block, axis, [(i, i ^ 1) for i in range(size)])
+
+
+def shift(block, axis, distance):
+    size = lax.axis_size(axis)
+    return lax.ppermute(block, axis, [(i, (i + distance) % size) for i in range(size)])
+
+
+def pick(block, index, axis):
+    return lax.dynamic_index_in_dim(block, index, axis, keepdims=False)
+
+
+def in_order(at, own, other, axis=0):
+    return jnp.stack(
+        [jnp.where(at == 0, own, other), jnp.where(at == 0, other, own)], axis=axis
+    )
+
+
+def spread(weight):
+    rows, _, _, cols = weight.shape
+    z, x, c = lax.axis_index("z"), lax.axis_index("x"), lax.axis_index("c")
+    planes = lax.axis_size("z")
+    own = jnp.moveaxis(pick(weight, c, 2), 1, 0)
+    other = swap(jnp.moveaxis(pick(weight, 1 - c, 2), 1, 0), "c")
+    block = in_order(c, own, other, axis=1).reshape(2, 2 * rows, cols)
+    pieces = [(z, pick(block, z % 2, 0))]
+    for distance in range(1, planes):
+        piece = pick(block, (z + distance) % 2, 0)
+        pieces.append(((z - distance + planes) % planes, shift(piece, "z", distance)))
+    whole = jnp.zeros((planes, 2, 2 * rows, cols), weight.dtype)
+    for place, piece in pieces:
+        across = swap(piece, "x")
+        whole = lax.dynamic_update_slice(whole, piece[None, None], (place, x, 0, 0))
+        whole = lax.dynamic_update_slice(whole, across[None, None], (place, 1 - x, 0, 0))
+    return whole.reshape(planes * 4 * rows, cols)
+
+
+def rearranged(
+    residual,
+    input_gain,
+    w_query,
+    key_weight,
+    value_weight,
+    query_gain,
+    key_gain,
+    w_out,
+    post_gain,
+    positions,
+):
+    tok, half_width = residual.shape
+    head_dim = query_gain.shape[0]
+    z, x, c = lax.axis_index("z"), lax.axis_index("x"), lax.axis_index("c")
+    y = lax.axis_index("y")
+    pair, zz = z // 2, z % 2
+    rows = w_query.shape[0]
+    kv_cols = key_weight.shape[1] // 4
+    q_cols = w_query.shape[1] // 4
+    kv_heads = kv_cols // head_dim
+    group = q_cols // kv_cols
+    run = 2 * tok
+    full_width = 2 * half_width
+
+    stream = residual.astype(jnp.float32)
+    squares = jnp.sum(stream * stream, axis=1, keepdims=True)
+    squares = squares + swap(squares, "y")
+    gain_in = lax.dynamic_slice_in_dim(input_gain, y * half_width, half_width, 0)
+    normed = (stream * lax.rsqrt(squares / full_width + epsilon) * gain_in).astype(jnp.bfloat16)
+    normed = in_order(zz, normed, swap(normed, "z"))
+    other = swap(normed, "y")
+    normed = jnp.concatenate(
+        [jnp.where(y == 0, normed, other), jnp.where(y == 0, other, normed)], axis=-1
+    )
+    normed = in_order(c, normed, swap(normed, "c"), axis=1).reshape(2 * run, full_width)
+
+    kv_weight = jnp.concatenate(
+        [
+            key_weight.reshape(rows, 2, 2, kv_cols),
+            value_weight.reshape(rows, 2, 2, kv_cols),
+        ],
+        axis=-1,
+    )
+    kv_all = spread(kv_weight)
+    q_all = spread(w_query.reshape(rows, 2, 2, q_cols))
+    o_all = spread(w_out.T.reshape(rows, 2, 2, q_cols))
+
+    def places_of(i):
+        return lax.dynamic_slice_in_dim(positions, (4 * pair + 2 * i + x) * run, run, 0)
+
+    places = jnp.concatenate([places_of(0), places_of(1)])
+    kv_raw = jnp.dot(normed, kv_all, preferred_element_type=jnp.float32)
+    keys = rotary(
+        norm_scale(kv_raw[:, :kv_cols].reshape(2 * run, kv_heads, head_dim), key_gain), places
+    ).reshape(2 * run, kv_cols)
+    kv = jnp.concatenate([keys, kv_raw[:, kv_cols:]], axis=1).astype(jnp.bfloat16)
+    kv = kv.reshape(2, run, 2 * kv_cols)
+    before = from_behind(kv[1], "z", 2)
+    own = jnp.concatenate([before[None], kv])
+    across = jnp.concatenate([swap(before, "x")[None], swap(kv, "x")])
+    kv_runs = in_order(x, own, across, axis=1).reshape(6 * run, 2 * kv_cols)
+    key_places = lax.dynamic_slice_in_dim(
+        jnp.concatenate([jnp.zeros((2 * run,), jnp.int32), positions]), 4 * pair * run, 6 * run, 0
+    )
+    key_index = (4 * pair - 2) * run + jnp.arange(6 * run, dtype=jnp.int32)
+    key_places = jnp.where(key_index >= 0, key_places, jnp.int32(1 << 30))
+
+    q_raw = jnp.dot(normed, q_all, preferred_element_type=jnp.float32)
+    queries = rotary(
+        norm_scale(q_raw.reshape(2 * run, kv_heads * group, head_dim), query_gain), places
+    ).astype(jnp.bfloat16)
+    queries = queries.reshape(2, run, kv_heads, group, head_dim)
+
+    def attend(i):
+        start = (2 * i + x) * run
+        window = lax.dynamic_slice_in_dim(kv_runs, start, 3 * run, 0)
+        window_places = lax.dynamic_slice_in_dim(key_places, start, 3 * run, 0)
+        window_keys = window[:, :kv_cols].reshape(3 * run, kv_heads, head_dim)
+        window_values = window[:, kv_cols:].reshape(3 * run, kv_heads, head_dim)
+        scores = (
+            jnp.einsum(
+                "qkgd,skd->kgqs", queries[i], window_keys, preferred_element_type=jnp.float32
+            )
+            * score_scale
+        )
+        distance = places_of(i)[:, None] - window_places[None, :]
+        allowed = (distance >= 0) & (distance < LOOKBACK_SPAN)
+        weights = jnp.where(allowed[None, None], jnp.exp(scores), jnp.zeros_like(scores))
+        total = jnp.sum(weights, axis=-1)
+        summed = jnp.einsum(
+            "kgqs,skd->qkgd",
+            weights.astype(jnp.bfloat16),
+            window_values,
+            preferred_element_type=jnp.float32,
+        )
+        merged = summed / jnp.transpose(total, (2, 0, 1))[..., None]
+        return merged.astype(jnp.bfloat16).reshape(run, q_cols)
+
+    attended = jnp.concatenate([attend(0), attend(1)])
+
+    cut = (half_width // 2 + 127) // 128 * 128
+    o_halves = o_all.reshape(2, half_width, q_cols)
+    sums = []
+    for low, high, z_first in ((0, cut, True), (cut, half_width, False)):
+        width = high - low
+        part = lax.dot_general(
+            attended,
+            o_halves[:, low:high].reshape(2 * width, q_cols),
+            (((1,), (1,)), ((), ())),
+            preferred_element_type=jnp.float32,
+        )
+        part = part.reshape(2, 2, tok, 2 * width)
+        part = pick(part, c, 1) + swap(pick(part, 1 - c, 1).astype(jnp.bfloat16), "c").astype(
+            jnp.float32
+        )
+        part = part.reshape(2, tok, 2, width)
+        for axis in ("z", "y") if z_first else ("y", "z"):
+            at, dim = (zz, 0) if axis == "z" else (y, part.ndim - 2)
+            part = pick(part, at, dim) + swap(
+                pick(part, 1 - at, dim).astype(jnp.bfloat16), axis
+            ).astype(jnp.float32)
+        sums.append(part)
+    attn_sum = jnp.concatenate(sums, axis=1)
+    squares = jnp.sum(attn_sum * attn_sum, axis=1, keepdims=True)
+    squares = squares + swap(squares, "y")
+    gain_out = lax.dynamic_slice_in_dim(post_gain, y * half_width, half_width, 0)
+    return (stream + attn_sum * lax.rsqrt(squares / full_width + epsilon) * gain_out).astype(
+        jnp.bfloat16
+    )
+
+
 def solution(mesh):
+    seq, tp = mesh.shape["seq"], mesh.shape["tp"]
+    if tp == 2 and seq % 8 == 0:
+        mesh = Mesh(mesh.devices.reshape(seq // 4, 2, 2, tp), ("z", "x", "c", "y"))
+        seq_axes, tp_axes, body = ("z", "x", "c"), "y", rearranged
+    else:
+        seq_axes, tp_axes, body = "seq", "tp", local
     in_specs = (
-        P("seq", "tp"),
-        P(),
-        P("seq", "tp"),
-        P("seq", "tp"),
-        P("seq", "tp"),
-        P(),
-        P(),
-        P("tp", "seq"),
-        P(),
-        P(),
-    )
-    out_specs = P("seq", "tp")
-    return jax.shard_map(local, mesh=mesh, in_specs=in_specs, out_specs=out_specs, check_vma=False)
+        P(seq_axes, tp_axes),
+        P(),
+        P(seq_axes, tp_axes),
+        P(seq_axes, tp_axes),
+        P(seq_axes, tp_axes),
+        P(),
+        P(),
+        P(tp_axes, seq_axes),
+        P(),
+        P(),
+    )
+    out_specs = P(seq_axes, tp_axes)
+    return jax.shard_map(body, mesh=mesh, in_specs=in_specs, out_specs=out_specs, check_vma=False)

time: 614 us -> 522 us (0.85); the launches traced: 613 us -> 512 us
  waiting for transfers between devices: 485 us -> 177 us
  starting transfers between devices: 12.4 us -> 122 us
  local copies, waits for them, and re-layouts: 25.8 us -> 120 us
  other arithmetic: 14.1 us -> 49.6 us
  matrix products: 56.6 us -> 42.4 us
  between operations: 13.8 us -> 1.55 us
    all_gather x5 -> x0, waiting for transfers between devices: 368 us -> none  [the longest x1 106 us: local(): lax.all_gather(w_out, 'seq', axis=1, tiled=True)]
    ppermute x0 -> x37, waiting for transfers between devices: none -> 177 us  [the longest x28 145 us: swap(): return lax.ppermute(block, axis, [(i, i ^ 1) for i in range(size)])]
    ppermute x0 -> x37, starting transfers between devices: none -> 119 us  [the longest x9 85.7 us: shift(): lax.ppermute(block, axis, [(i, (i + distance) % size) for i in range(size)])]
    ppermute x4 -> x1, waiting for transfers between devices: 75.9 us -> 0.01 us  [from_behind(): return lax.ppermute(block, axis, route)]
    unnamed x7 -> x0, waiting for transfers between devices: 41.5 us -> none
    dynamic_slice x2 -> x14, local copies, waits for them, and re-layouts: 0.15 us -> 28.6 us  [the longest x10 28.3 us: pick(): return lax.dynamic_index_in_dim(block, index, axis, keepdims=False)]
    reshape x0 -> x6, local copies, waits for them, and re-layouts: none -> 26 us  [the longest x2 15.6 us: rearranged(): part = part.reshape(2, tok, 2, width)]
    dynamic_update_slice x0 -> x24, local copies, waits for them, and re-layouts: none -> 22.5 us  [the longest x12 12.2 us: spread(): lax.dynamic_update_slice(whole, across[None, None], (place, 1 - x, 0, 0))]
  transfers between devices with their start and end apart: 10 -> 38, of which waited for: 9 -> 18; matrix products, arithmetic and copies ran while one was open for 12% -> 29% of each run, Pallas kernels for 0% -> 0%
where the time goes in v1:
time: 522 us; the launch traced here: 512 us
  waiting for transfers between devices  177 us (34%)
  starting transfers between devices  122 us (23%)
  local copies, waits for them, and re-layouts  120 us (23%)
  other arithmetic  49.6 us (10%)
  matrix products  42.4 us (8%)
    ppermute x28, waiting for transfers between devices, swap(): return lax.ppermute(block, axis, [(i, i ^ 1) for i in range(size)])  145 us
    ppermute x9, starting transfers between devices, shift(): lax.ppermute(block, axis, [(i, (i + distance) % size) for i in range(size)])  85.7 us
    ppermute x28, starting transfers between devices, swap(): return lax.ppermute(block, axis, [(i, i ^ 1) for i in range(size)])  33.1 us
    ppermute x9, waiting for transfers between devices, shift(): lax.ppermute(block, axis, [(i, (i + distance) % size) for i in range(size)])  31.9 us
    dynamic_slice x10, local copies, waits for them, and re-layouts, pick(): return lax.dynamic_index_in_dim(block, index, axis, keepdims=False)  28.3 us
    reshape x2, local copies, waits for them, and re-layouts, rearranged(): part = part.reshape(2, tok, 2, width)  15.6 us
    another operation x10, other arithmetic, in_order(): jnp.stack([jnp.where(at == 0, own, other), jnp.where(at == 0, other, own)...  14 us
    add x2, other arithmetic, rearranged(): pick(part, c, 1)  12.9 us
  transfers between devices with their start and end apart: 38, of which 18 were waited for; matrix products, arithmetic and copies ran while one was open for 29% of the time, Pallas kernels for 0%

profile of v1, /device:TPU:0, one launch (start us, length us, event | category | flops | bytes accessed | tf_op | source)
XLA Modules:
  0.0 512.3 jit_solution(4600359546079867620)
XLA Ops:
  20.8 4.0 constant_dynamic-slice_fusion.5
  34.8 6.5 %collective-permute-done.1 = bf16[256,2688]{1,0:T(8,128)(2,1)} collective-permute-done((bf16[256,2688]{1,0:T(8,128)(2,1)}, bf16[256,2688]{1,0:T(8,128)(2,1)}, u32[]{:S(2)}, u32[]{:S(2)}) %collective-permute-start.1) | collective-permute-done | bytes 1376288 | tf_op jit(solution)/shard_map/ppermute | solution.py:140
  66.8 39.0 %collective-permute-done.2 = bf16[2,256,2688]{2,1,0:T(8,128)(2,1)} collective-permute-done((bf16[2,256,2688]{2,1,0:T(8,128)(2,1)}, bf16[2,256,2688]{2,1,0:T(8,128)(2,1)}, u32[]{:S(2)}, u32[]{:S(2)}) %collective-permute-start.2) | collective-permute-done | bytes 2752544 | tf_op jit(solution)/shard_map/ppermute | solution.py:140
  123.3 6.7 %collective-permute-done.16 = bf16[672,512]{1,0:T(8,128)(2,1)S(1)} collective-permute-done((bf16[672,512]{1,0:T(8,128)(2,1)S(1)}, bf16[672,512]{1,0:T(8,128)(2,1)S(1)}, u32[]{:S(2)}, u32[]{:S(2)}) %collective-permute-start.16) | collective-permute-done | bytes 688160 | tf_op jit(solution)/shard_map/ppermute | solution.py:140
  135.6 37.5 %collective-permute-start.19 = (bf16[672,512]{1,0:T(8,128)(2,1)S(1)}, bf16[672,512]{1,0:T(8,128)(2,1)S(1)}, u32[]{:S(2)}, u32[]{:S(2)}) collective-permute-start(bf16[672,512]{1,0:T(8,128)(2,1)S(1)} %get-tuple-element.35), channel_id=1, source_target_pairs={{0,16},{8,24},{16,0},{24,8},{1,17},{9,25},{17,1},{25,9},{2,18},{10... | collective-permute-start | bytes 2064392 | tf_op jit(solution)/shard_map/ppermute | solution.py:145
  174.6 23.0 %collective-permute-start.21 = (bf16[672,512]{1,0:T(8,128)(2,1)S(1)}, bf16[672,512]{1,0:T(8,128)(2,1)S(1)}, u32[]{:S(2)}, u32[]{:S(2)}) collective-permute-start(bf16[672,512]{1,0:T(8,128)(2,1)S(1)} %get-tuple-element.33), channel_id=1, source_target_pairs={{0,24},{8,0},{16,8},{24,16},{1,25},{9,1},{17,9},{25,17},{2,26},{10... | collective-permute-start | bytes 2064392 | tf_op jit(solution)/shard_map/ppermute | solution.py:145
  199.9 8.3 %collective-permute-done.19 = bf16[672,512]{1,0:T(8,128)(2,1)S(1)} collective-permute-done((bf16[672,512]{1,0:T(8,128)(2,1)S(1)}, bf16[672,512]{1,0:T(8,128)(2,1)S(1)}, u32[]{:S(2)}, u32[]{:S(2)}) %collective-permute-start.19) | collective-permute-done | bytes 688160 | tf_op jit(solution)/shard_map/ppermute | solution.py:145
  208.2 14.7 %collective-permute-done.21 = bf16[672,512]{1,0:T(8,128)(2,1)S(1)} collective-permute-done((bf16[672,512]{1,0:T(8,128)(2,1)S(1)}, bf16[672,512]{1,0:T(8,128)(2,1)S(1)}, u32[]{:S(2)}, u32[]{:S(2)}) %collective-permute-start.21) | collective-permute-done | bytes 688160 | tf_op jit(solution)/shard_map/ppermute | solution.py:145
  222.9 16.3 %collective-permute-start.10 = (bf16[672,512]{1,0:T(8,128)(2,1)S(1)}, bf16[672,512]{1,0:T(8,128)(2,1)}, u32[]{:S(2)}, u32[]{:S(2)}) collective-permute-start(bf16[672,512]{1,0:T(8,128)(2,1)S(1)} %get-tuple-element.39), channel_id=1, source_target_pairs={{0,24},{8,0},{16,8},{24,16},{1,25},{9,1},{17,9},{25,17},{2,26},{10... | collective-permute-start | bytes 2064392 | tf_op jit(solution)/shard_map/ppermute | solution.py:145
  247.1 7.0 %collective-permute-done.10 = bf16[672,512]{1,0:T(8,128)(2,1)} collective-permute-done((bf16[672,512]{1,0:T(8,128)(2,1)S(1)}, bf16[672,512]{1,0:T(8,128)(2,1)}, u32[]{:S(2)}, u32[]{:S(2)}) %collective-permute-start.10) | collective-permute-done | bytes 688160 | tf_op jit(solution)/shard_map/ppermute | solution.py:145
  259.9 12.4 %collective-permute-done.22 = bf16[672,512]{1,0:T(8,128)(2,1)S(1)} collective-permute-done((bf16[672,512]{1,0:T(8,128)(2,1)S(1)}, bf16[672,512]{1,0:T(8,128)(2,1)S(1)}, u32[]{:S(2)}, u32[]{:S(2)}) %collective-permute-start.22) | collective-permute-done | bytes 688160 | tf_op jit(solution)/shard_map/ppermute | solution.py:140
  273.3 8.4 %copy.97 = bf16[512,5376]{1,0:T(8,128)(2,1)} copy(bf16[512,5376]{0,1:T(8,128)(2,1)} %bitcast.64) | data formatting | bytes 11010048 | tf_op jit(solution)/shard_map/dot_general | solution.py:245
  281.6 5.5 %collective-permute-done.7 = bf16[672,512]{1,0:T(8,128)(2,1)} collective-permute-done((bf16[672,512]{1,0:T(8,128)(2,1)}, bf16[672,512]{1,0:T(8,128)(2,1)}, u32[]{:S(2)}, u32[]{:S(2)}) %collective-permute-start.7) | collective-permute-done | bytes 688160 | tf_op jit(solution)/shard_map/ppermute | solution.py:140
  291.3 10.6 %collective-permute-done.9 = bf16[672,512]{1,0:T(8,128)(2,1)} collective-permute-done((bf16[672,512]{1,0:T(8,128)(2,1)}, bf16[672,512]{1,0:T(8,128)(2,1)}, u32[]{:S(2)}, u32[]{:S(2)}) %collective-permute-start.9) | collective-permute-done | bytes 688160 | tf_op jit(solution)/shard_map/ppermute | solution.py:140
  305.9 8.3 %collective-permute-done.11 = bf16[672,512]{1,0:T(8,128)(2,1)} collective-permute-done((bf16[672,512]{1,0:T(8,128)(2,1)}, bf16[672,512]{1,0:T(8,128)(2,1)}, u32[]{:S(2)}, u32[]{:S(2)}) %collective-permute-start.11) | collective-permute-done | bytes 688160 | tf_op jit(solution)/shard_map/ppermute | solution.py:140
  316.2 5.3 %select_bitcast_fusion.1 = (bf16[2,1,256,5376]{3,2,0,1:T(8,128)(2,1)S(1)}, bf16[2,1,256,5376]{3,2,0,1:T(8,128)(2,1)S(1)}) fusion(bf16[2,256,5376]{2,1,0:T(8,128)(2,1)} %collective-permute-done.3, pred[]{:T(512)S(6)} %eq.46, bf16[2,256,2688]{2,1,0:T(8,128)(2,1)S(1)} %copy-done.1, bf16[2,256,2688]{2,1,0:T(8,128)(2,1)S(1)} %get-tuple-element.7), kind=kLoop, calls=%fused_computation.19 | loop fusion | flops 16515072 | bytes 22020096 | tf_op jit(solution)/shard_map/stack | solution.py:153
  324.2 10.0 %fusion.51 = f32[1024,512]{0,1:T(8,128)S(1)} fusion(bf16[1024,5376]{1,0:T(8,128)(2,1)S(1)} %bitcast.284, bf16[5376,512]{1,0:T(8,128)(2,1)} %bitcast.287), kind=kOutput, calls=%fused_computation.168 | convolution fusion | flops 5637144576 | bytes 18612224 | tf_op jit(solution)/shard_map/dot_general | solution.py:229
  344.0 10.5 %multiply_reduce_fusion.1 = (f32[1024,4]{0,1:T(4,128)S(1)}, f32[1024,4,128]{0,2,1:T(8,128)S(1)}) fusion(bf16[1024,5376,1]{1,0,2:T(8,128)(2,1)} %bitcast.285, bf16[4,128,5376]{2,1,0:T(8,128)(2,1)} %bitcast.286), kind=kOutput, calls=%fused_computation.48 | convolution fusion | flops 5638189056 | bytes 18628608 | tf_op jit(solution)/shard_map/dot_general | solution.py:245
  358.2 15.8 %collective-permute-done.13 = bf16[512,512]{0,1:T(8,128)(2,1)} collective-permute-done((bf16[512,512]{0,1:T(8,128)(2,1)S(1)}, bf16[512,512]{0,1:T(8,128)(2,1)}, u32[]{:S(2)}, u32[]{:S(2)}) %collective-permute-start.13) | collective-permute-done | bytes 524320 | tf_op jit(solution)/shard_map/ppermute | solution.py:140
  380.3 4.9 fusion.2
  395.1 4.7 fusion.53
  408.3 4.2 copy-done.9
  412.9 6.4 %bitcast_add_fusion.1 = f32[2,256,2560]{2,1,0:T(8,128)} fusion(bf16[2,256,2560]{2,1,0:T(8,128)(2,1)} %collective-permute-done.34, f32[2,2,256,2560]{3,2,1,0:T(8,128)} %copy-done.10, s32[]{:T(128)S(6)} %select_n.318), kind=kLoop, calls=%fused_computation.20 | loop fusion | flops 2621440 | bytes 13107204 | tf_op jit(solution)/shard_map/add | solution.py:290
  419.3 7.5 %reshape.408 = f32[2,256,2,1280]{3,2,1,0:T(2,128)} reshape(f32[2,256,2560]{2,1,0:T(8,128)} %bitcast_add_fusion.1) | data formatting | bytes 10485760 | tf_op jit(solution)/shard_map/reshape | solution.py:293
  426.8 4.8 constant_dynamic-slice_fusion
  433.4 6.5 %bitcast_add_fusion = f32[2,256,2816]{2,1,0:T(8,128)} fusion(bf16[2,256,2816]{2,1,0:T(8,128)(2,1)} %collective-permute-done.31, f32[2,2,256,2816]{3,2,1,0:T(8,128)} %copy-done.9, s32[]{:T(128)S(6)} %select_n.318), kind=kLoop, calls=%fused_computation.15 | loop fusion | flops 2883584 | bytes 14417924 | tf_op jit(solution)/shard_map/add | solution.py:290
  439.8 8.1 %reshape.406 = f32[2,256,2,1408]{3,2,1,0:T(2,128)} reshape(f32[2,256,2816]{2,1,0:T(8,128)} %bitcast_add_fusion) | data formatting | bytes 11534336 | tf_op jit(solution)/shard_map/reshape | solution.py:293
  451.0 5.1 collective-permute-start.32
  456.1 5.2 %constant_dynamic-slice_fusion.1 = f32[2,256,1,1280]{3,2,1,0:T(1,128)S(1)} fusion(f32[2,256,2,1280]{3,2,1,0:T(2,128)} %reshape.408, s32[]{:T(128)S(6)} %select_n.354), kind=kLoop, calls=%fused_computation.141 | loop fusion | bytes 5242884 | tf_op jit(solution)/shard_map/jit(dynamic_index_in_dim)/dynamic_slice | solution.py:149
  466.0 5.1 collective-permute-start.36
  471.1 17.4 %collective-permute-done.32 = bf16[256,2,1408]{2,0,1:T(8,128)(2,1)S(1)} collective-permute-done((bf16[256,2,1408]{2,0,1:T(8,128)(2,1)S(1)}, bf16[256,2,1408]{2,0,1:T(8,128)(2,1)S(1)}, u32[]{:S(2)}, u32[]{:S(2)}) %collective-permute-start.32) | collective-permute-done | bytes 1441824 | tf_op jit(solution)/shard_map/ppermute | solution.py:140
  490.5 11.6 %collective-permute-done.36 = bf16[256,1280]{1,0:T(8,128)(2,1)S(1)} collective-permute-done((bf16[256,1280]{1,0:T(8,128)(2,1)S(1)}, bf16[256,1280]{1,0:T(8,128)(2,1)S(1)}, u32[]{:S(2)}, u32[]{:S(2)}) %collective-permute-start.36) | collective-permute-done | bytes 655392 | tf_op jit(solution)/shard_map/ppermute | solution.py:140
  (236 shorter events, 169.6 us)
Async XLA Ops:
  9.3 32.0 %collective-permute-start.1 = (bf16[256,2688]{1,0:T(8,128)(2,1)}, bf16[256,2688]{1,0:T(8,128)(2,1)}, u32[]{:S(2)}, u32[]{:S(2)}) collective-permute-start(bf16[256,2688]{1,0:T(8,128)(2,1)} %fusion.19), channel_id=1, source_target_pairs={{0,8},{8,0},{16,24},{24,16},{1,9},{9,1},{17,25},{25,17},{2,10},{10... | collective-permute-start | bytes 4128776 | tf_op jit(solution)/shard_map/ppermute | solution.py:140
  17.1 32.3 %collective-permute-start.4 = (bf16[2,336,512]{2,1,0:T(8,128)(2,1)}, bf16[2,336,512]{2,1,0:T(8,128)(2,1)}, u32[]{:S(2)}, u32[]{:S(2)}) collective-permute-start(bf16[2,336,512]{2,1,0:T(8,128)(2,1)} %bitcast.272), channel_id=1, source_target_pairs={{0,2},{2,0},{1,3},{3,1},{4,6},{6,4},{5,7},{7,5},{8,10},{10,8},{9,1... | collective-permute-start | bytes 2064392 | tf_op jit(solution)/shard_map/ppermute | solution.py:140
  25.9 29.4 %collective-permute-start.23 = (bf16[2,336,512]{2,1,0:T(8,128)(2,1)}, bf16[2,336,512]{2,1,0:T(8,128)(2,1)}, u32[]{:S(2)}, u32[]{:S(2)}) collective-permute-start(bf16[2,336,512]{2,1,0:T(8,128)(2,1)} %bitcast.270), channel_id=1, source_target_pairs={{0,2},{2,0},{1,3},{3,1},{4,6},{6,4},{5,7},{7,5},{8,10},{10,8},{9,1... | collective-permute-start | bytes 2064392 | tf_op jit(solution)/shard_map/ppermute | solution.py:140
  34.5 20.9 %collective-permute-start.15 = (bf16[2,336,512]{2,1,0:T(8,128)(2,1)S(1)}, bf16[2,336,512]{2,1,0:T(8,128)(2,1)S(1)}, u32[]{:S(2)}, u32[]{:S(2)}) collective-permute-start(bf16[2,336,512]{2,1,0:T(8,128)(2,1)S(1)} %bitcast.300), channel_id=1, source_target_pairs={{0,2},{2,0},{1,3},{3,1},{4,6},{6,4},{5,7},{7,5},{8,10},{10,8},{9,1... | collective-permute-start | bytes 2064392 | tf_op jit(solution)/shard_map/ppermute | solution.py:140
  45.3 60.5 %collective-permute-start.2 = (bf16[2,256,2688]{2,1,0:T(8,128)(2,1)}, bf16[2,256,2688]{2,1,0:T(8,128)(2,1)}, u32[]{:S(2)}, u32[]{:S(2)}) collective-permute-start(bf16[2,256,2688]{2,1,0:T(8,128)(2,1)} %pad_maximum_fusion.3), channel_id=1, source_target_pairs={{0,1},{1,0},{2,3},{3,2},{4,5},{5,4},{6,7},{7,6},{8,9},{9,8},{10,11... | collective-permute-start | bytes 8257544 | tf_op jit(solution)/shard_map/ppermute | solution.py:140
  52.1 60.0 %collective-permute-start.5 = (bf16[672,512]{1,0:T(8,128)(2,1)}, bf16[672,512]{1,0:T(8,128)(2,1)}, u32[]{:S(2)}, u32[]{:S(2)}) collective-permute-start(bf16[672,512]{1,0:T(8,128)(2,1)} %get-tuple-element.40), channel_id=1, source_target_pairs={{0,4},{4,0},{1,5},{5,1},{2,6},{6,2},{3,7},{7,3},{8,12},{12,8},{9,1... | collective-permute-start | bytes 2064392 | tf_op jit(solution)/shard_map/ppermute | solution.py:140
  53.8 68.1 %collective-permute-start.6 = (bf16[672,512]{1,0:T(8,128)(2,1)S(1)}, bf16[672,512]{1,0:T(8,128)(2,1)}, u32[]{:S(2)}, u32[]{:S(2)}) collective-permute-start(bf16[672,512]{1,0:T(8,128)(2,1)S(1)} %get-tuple-element.42), channel_id=1, source_target_pairs={{0,8},{8,16},{16,24},{24,0},{1,9},{9,17},{17,25},{25,1},{2,10},{10... | collective-permute-start | bytes 2064392 | tf_op jit(solution)/shard_map/ppermute | solution.py:145
  59.0 56.3 %collective-permute-start.24 = (bf16[672,512]{1,0:T(8,128)(2,1)}, bf16[672,512]{1,0:T(8,128)(2,1)}, u32[]{:S(2)}, u32[]{:S(2)}) collective-permute-start(bf16[672,512]{1,0:T(8,128)(2,1)} %get-tuple-element.28), channel_id=1, source_target_pairs={{0,4},{4,0},{1,5},{5,1},{2,6},{6,2},{3,7},{7,3},{8,12},{12,8},{9,1... | collective-permute-start | bytes 2064392 | tf_op jit(solution)/shard_map/ppermute | solution.py:140
  59.5 58.6 %collective-permute-start.25 = (bf16[672,512]{1,0:T(8,128)(2,1)}, bf16[672,512]{1,0:T(8,128)(2,1)}, u32[]{:S(2)}, u32[]{:S(2)}) collective-permute-start(bf16[672,512]{1,0:T(8,128)(2,1)} %get-tuple-element.30), channel_id=1, source_target_pairs={{0,8},{8,16},{16,24},{24,0},{1,9},{9,17},{17,25},{25,1},{2,10},{10... | collective-permute-start | bytes 2064392 | tf_op jit(solution)/shard_map/ppermute | solution.py:145
  111.5 204.7 %collective-permute-start.3 = (bf16[2,256,5376]{2,1,0:T(8,128)(2,1)}, bf16[2,256,5376]{2,1,0:T(8,128)(2,1)}, u32[]{:S(2)}, u32[]{:S(2)}) collective-permute-start(bf16[2,256,5376]{2,1,0:T(8,128)(2,1)} %pad_maximum_fusion.1), channel_id=1, source_target_pairs={{0,2},{2,0},{1,3},{3,1},{4,6},{6,4},{5,7},{7,5},{8,10},{10,8},{9,1... | collective-permute-start | bytes 16515080 | tf_op jit(solution)/shard_map/ppermute | solution.py:140
  115.3 20.3 %collective-permute-start.17 = (bf16[672,512]{1,0:T(8,128)(2,1)S(1)}, bf16[672,512]{1,0:T(8,128)(2,1)S(1)}, u32[]{:S(2)}, u32[]{:S(2)}) collective-permute-start(bf16[672,512]{1,0:T(8,128)(2,1)S(1)} %copy-done.21), channel_id=1, source_target_pairs={{0,8},{8,16},{16,24},{24,0},{1,9},{9,17},{17,25},{25,1},{2,10},{10... | collective-permute-start | bytes 2064392 | tf_op jit(solution)/shard_map/ppermute | solution.py:145
  118.1 55.0 %collective-permute-start.27 = (bf16[672,512]{1,0:T(8,128)(2,1)S(1)}, bf16[672,512]{1,0:T(8,128)(2,1)S(1)}, u32[]{:S(2)}, u32[]{:S(2)}) collective-permute-start(bf16[672,512]{1,0:T(8,128)(2,1)S(1)} %copy-done.20), channel_id=1, source_target_pairs={{0,16},{8,24},{16,0},{24,8},{1,17},{9,25},{17,1},{25,9},{2,18},{10... | collective-permute-start | bytes 2064392 | tf_op jit(solution)/shard_map/ppermute | solution.py:145
  121.9 52.7 %collective-permute-start.29 = (bf16[672,512]{1,0:T(8,128)(2,1)S(1)}, bf16[672,512]{1,0:T(8,128)(2,1)S(1)}, u32[]{:S(2)}, u32[]{:S(2)}) collective-permute-start(bf16[672,512]{1,0:T(8,128)(2,1)S(1)} %get-tuple-element.27), channel_id=1, source_target_pairs={{0,24},{8,0},{16,8},{24,16},{1,25},{9,1},{17,9},{25,17},{2,26},{10... | collective-permute-start | bytes 2064392 | tf_op jit(solution)/shard_map/ppermute | solution.py:145
  130.0 67.6 %collective-permute-start.26 = (bf16[672,512]{1,0:T(8,128)(2,1)}, bf16[672,512]{1,0:T(8,128)(2,1)S(1)}, u32[]{:S(2)}, u32[]{:S(2)}) collective-permute-start(bf16[672,512]{1,0:T(8,128)(2,1)} %collective-permute-done.25), channel_id=1, source_target_pairs={{0,4},{4,0},{1,5},{5,1},{2,6},{6,2},{3,7},{7,3},{8,12},{12,8},{9,1... | collective-permute-start | bytes 2064392 | tf_op jit(solution)/shard_map/ppermute | solution.py:140
  135.6 72.6 %collective-permute-start.19 = (bf16[672,512]{1,0:T(8,128)(2,1)S(1)}, bf16[672,512]{1,0:T(8,128)(2,1)S(1)}, u32[]{:S(2)}, u32[]{:S(2)}) collective-permute-start(bf16[672,512]{1,0:T(8,128)(2,1)S(1)} %get-tuple-element.35), channel_id=1, source_target_pairs={{0,16},{8,24},{16,0},{24,8},{1,17},{9,25},{17,1},{25,9},{2,18},{10... | collective-permute-start | bytes 2064392 | tf_op jit(solution)/shard_map/ppermute | solution.py:145
  173.1 26.1 %collective-permute-start.28 = (bf16[672,512]{1,0:T(8,128)(2,1)S(1)}, bf16[672,512]{1,0:T(8,128)(2,1)S(1)}, u32[]{:S(2)}, u32[]{:S(2)}) collective-permute-start(bf16[672,512]{1,0:T(8,128)(2,1)S(1)} %collective-permute-done.27), channel_id=1, source_target_pairs={{0,4},{4,0},{1,5},{5,1},{2,6},{6,2},{3,7},{7,3},{8,12},{12,8},{9,1... | collective-permute-start | bytes 2064392 | tf_op jit(solution)/shard_map/ppermute | solution.py:140
  174.6 48.3 %collective-permute-start.21 = (bf16[672,512]{1,0:T(8,128)(2,1)S(1)}, bf16[672,512]{1,0:T(8,128)(2,1)S(1)}, u32[]{:S(2)}, u32[]{:S(2)}) collective-permute-start(bf16[672,512]{1,0:T(8,128)(2,1)S(1)} %get-tuple-element.33), channel_id=1, source_target_pairs={{0,24},{8,0},{16,8},{24,16},{1,25},{9,1},{17,9},{25,17},{2,26},{10... | collective-permute-start | bytes 2064392 | tf_op jit(solution)/shard_map/ppermute | solution.py:145
  197.6 41.6 %collective-permute-start.30 = (bf16[672,512]{1,0:T(8,128)(2,1)S(1)}, bf16[672,512]{1,0:T(8,128)(2,1)S(1)}, u32[]{:S(2)}, u32[]{:S(2)}) collective-permute-start(bf16[672,512]{1,0:T(8,128)(2,1)S(1)} %collective-permute-done.29), channel_id=1, source_target_pairs={{0,4},{4,0},{1,5},{5,1},{2,6},{6,2},{3,7},{7,3},{8,12},{12,8},{9,1... | collective-permute-start | bytes 2064392 | tf_op jit(solution)/shard_map/ppermute | solution.py:140
  199.2 44.0 %collective-permute-start.18 = (bf16[672,512]{1,0:T(8,128)(2,1)S(1)}, bf16[672,512]{1,0:T(8,128)(2,1)S(1)}, u32[]{:S(2)}, u32[]{:S(2)}) collective-permute-start(bf16[672,512]{1,0:T(8,128)(2,1)S(1)} %collective-permute-done.17), channel_id=1, source_target_pairs={{0,4},{4,0},{1,5},{5,1},{2,6},{6,2},{3,7},{7,3},{8,12},{12,8},{9,1... | collective-permute-start | bytes 2064392 | tf_op jit(solution)/shard_map/ppermute | solution.py:140
  208.2 38.3 %collective-permute-start.8 = (bf16[672,512]{1,0:T(8,128)(2,1)S(1)}, bf16[672,512]{1,0:T(8,128)(2,1)}, u32[]{:S(2)}, u32[]{:S(2)}) collective-permute-start(bf16[672,512]{1,0:T(8,128)(2,1)S(1)} %get-tuple-element.41), channel_id=1, source_target_pairs={{0,16},{8,24},{16,0},{24,8},{1,17},{9,25},{17,1},{25,9},{2,18},{10... | collective-permute-start | bytes 2064392 | tf_op jit(solution)/shard_map/ppermute | solution.py:145
  222.9 31.2 %collective-permute-start.10 = (bf16[672,512]{1,0:T(8,128)(2,1)S(1)}, bf16[672,512]{1,0:T(8,128)(2,1)}, u32[]{:S(2)}, u32[]{:S(2)}) collective-permute-start(bf16[672,512]{1,0:T(8,128)(2,1)S(1)} %get-tuple-element.39), channel_id=1, source_target_pairs={{0,24},{8,0},{16,8},{24,16},{1,25},{9,1},{17,9},{25,17},{2,26},{10... | collective-permute-start | bytes 2064392 | tf_op jit(solution)/shard_map/ppermute | solution.py:145
  239.2 18.4 %collective-permute-start.20 = (bf16[672,512]{1,0:T(8,128)(2,1)S(1)}, bf16[672,512]{1,0:T(8,128)(2,1)S(1)}, u32[]{:S(2)}, u32[]{:S(2)}) collective-permute-start(bf16[672,512]{1,0:T(8,128)(2,1)S(1)} %collective-permute-done.19), channel_id=1, source_target_pairs={{0,4},{4,0},{1,5},{5,1},{2,6},{6,2},{3,7},{7,3},{8,12},{12,8},{9,1... | collective-permute-start | bytes 2064392 | tf_op jit(solution)/shard_map/ppermute | solution.py:140
  243.2 29.0 %collective-permute-start.22 = (bf16[672,512]{1,0:T(8,128)(2,1)S(1)}, bf16[672,512]{1,0:T(8,128)(2,1)S(1)}, u32[]{:S(2)}, u32[]{:S(2)}) collective-permute-start(bf16[672,512]{1,0:T(8,128)(2,1)S(1)} %collective-permute-done.21), channel_id=1, source_target_pairs={{0,4},{4,0},{1,5},{5,1},{2,6},{6,2},{3,7},{7,3},{8,12},{12,8},{9,1... | collective-permute-start | bytes 2064392 | tf_op jit(solution)/shard_map/ppermute | solution.py:140
  246.5 40.6 %collective-permute-start.7 = (bf16[672,512]{1,0:T(8,128)(2,1)}, bf16[672,512]{1,0:T(8,128)(2,1)}, u32[]{:S(2)}, u32[]{:S(2)}) collective-permute-start(bf16[672,512]{1,0:T(8,128)(2,1)} %collective-permute-done.6), channel_id=1, source_target_pairs={{0,4},{4,0},{1,5},{5,1},{2,6},{6,2},{3,7},{7,3},{8,12},{12,8},{9,1... | collective-permute-start | bytes 2064392 | tf_op jit(solution)/shard_map/ppermute | solution.py:140
  254.0 47.9 %collective-permute-start.9 = (bf16[672,512]{1,0:T(8,128)(2,1)}, bf16[672,512]{1,0:T(8,128)(2,1)}, u32[]{:S(2)}, u32[]{:S(2)}) collective-permute-start(bf16[672,512]{1,0:T(8,128)(2,1)} %collective-permute-done.8), channel_id=1, source_target_pairs={{0,4},{4,0},{1,5},{5,1},{2,6},{6,2},{3,7},{7,3},{8,12},{12,8},{9,1... | collective-permute-start | bytes 2064392 | tf_op jit(solution)/shard_map/ppermute | solution.py:140
  257.5 56.7 %collective-permute-start.11 = (bf16[672,512]{1,0:T(8,128)(2,1)}, bf16[672,512]{1,0:T(8,128)(2,1)}, u32[]{:S(2)}, u32[]{:S(2)}) collective-permute-start(bf16[672,512]{1,0:T(8,128)(2,1)} %collective-permute-done.10), channel_id=1, source_target_pairs={{0,4},{4,0},{1,5},{5,1},{2,6},{6,2},{3,7},{7,3},{8,12},{12,8},{9,1... | collective-permute-start | bytes 2064392 | tf_op jit(solution)/shard_map/ppermute | solution.py:140
  339.7 35.6 %collective-permute-start.14 = (bf16[2,512,512]{2,1,0:T(8,128)(2,1)}, bf16[2,512,512]{2,1,0:T(8,128)(2,1)}, u32[]{:S(2)}, u32[]{:S(2)}) collective-permute-start(bf16[2,512,512]{2,1,0:T(8,128)(2,1)} %get-tuple-element.48), channel_id=1, source_target_pairs={{0,4},{4,0},{1,5},{5,1},{2,6},{6,2},{3,7},{7,3},{8,12},{12,8},{9,1... | collective-permute-start | bytes 3145736 | tf_op jit(solution)/shard_map/ppermute | solution.py:140
  354.5 19.5 %collective-permute-start.13 = (bf16[512,512]{0,1:T(8,128)(2,1)S(1)}, bf16[512,512]{0,1:T(8,128)(2,1)}, u32[]{:S(2)}, u32[]{:S(2)}) collective-permute-start(bf16[512,512]{0,1:T(8,128)(2,1)S(1)} %collective-permute-done.12), channel_id=1, source_target_pairs={{0,4},{4,0},{1,5},{5,1},{2,6},{6,2},{3,7},{7,3},{8,12},{12,8},{9,1... | collective-permute-start | bytes 1572872 | tf_op jit(solution)/shard_map/ppermute | solution.py:140
  412.8 20.6 %collective-permute-start.31 = (bf16[2,256,2816]{2,1,0:T(8,128)(2,1)S(1)}, bf16[2,256,2816]{2,1,0:T(8,128)(2,1)}, u32[]{:S(2)}, u32[]{:S(2)}) collective-permute-start(bf16[2,256,2816]{2,1,0:T(8,128)(2,1)S(1)} %fusion.16), channel_id=1, source_target_pairs={{0,2},{2,0},{1,3},{3,1},{4,6},{6,4},{5,7},{7,5},{8,10},{10,8},{9,1... | collective-permute-start | bytes 8650760 | tf_op jit(solution)/shard_map/ppermute | solution.py:140
  432.9 31.5 %collective-permute-start.35 = (bf16[2,256,1280]{2,1,0:T(8,128)(2,1)}, bf16[2,256,1280]{2,1,0:T(8,128)(2,1)}, u32[]{:S(2)}, u32[]{:S(2)}) collective-permute-start(bf16[2,256,1280]{2,1,0:T(8,128)(2,1)} %bitcast.269), channel_id=1, source_target_pairs={{0,1},{1,0},{2,3},{3,2},{4,5},{5,4},{6,7},{7,6},{8,9},{9,8},{10,11... | collective-permute-start | bytes 3932168 | tf_op jit(solution)/shard_map/ppermute | solution.py:140
  451.0 37.5 %collective-permute-start.32 = (bf16[256,2,1408]{2,0,1:T(8,128)(2,1)S(1)}, bf16[256,2,1408]{2,0,1:T(8,128)(2,1)S(1)}, u32[]{:S(2)}, u32[]{:S(2)}) collective-permute-start(bf16[256,2,1408]{2,0,1:T(8,128)(2,1)S(1)} %bitcast.292), channel_id=1, source_target_pairs={{0,8},{8,0},{16,24},{24,16},{1,9},{9,1},{17,25},{25,17},{2,10},{10... | collective-permute-start | bytes 4325384 | tf_op jit(solution)/shard_map/ppermute | solution.py:140
  466.0 36.1 %collective-permute-start.36 = (bf16[256,1280]{1,0:T(8,128)(2,1)S(1)}, bf16[256,1280]{1,0:T(8,128)(2,1)S(1)}, u32[]{:S(2)}, u32[]{:S(2)}) collective-permute-start(bf16[256,1280]{1,0:T(8,128)(2,1)S(1)} %fusion.41), channel_id=1, source_target_pairs={{0,8},{8,0},{16,24},{24,16},{1,9},{9,1},{17,25},{25,17},{2,10},{10... | collective-permute-start | bytes 1966088 | tf_op jit(solution)/shard_map/ppermute | solution.py:140
  (38 other events, 400.8 us)

commit v2 on v1

--- a/solution.py
+++ b/solution.py
@@ -1,6 +1,10 @@
+import functools
+
 import jax
 import jax.numpy as jnp
 from jax import lax
+from jax.experimental import pallas as pl
+from jax.experimental.pallas import tpu as pltpu
 from jax.sharding import Mesh
 from jax.sharding import PartitionSpec as P
 
@@ -155,23 +159,233 @@
     )
 
 
-def spread(weight):
-    rows, _, _, cols = weight.shape
+def gather_kernel(
+    planes,
+    x_ref,
+    wk_ref,
+    wv_ref,
+    wq_ref,
+    wo_ref,
+    kv_ref,
+    q_ref,
+    o_ref,
+    x_all,
+    kv_all,
+    q_all,
+    x_send,
+    x_recv,
+    w_send,
+    w_recv,
+    f_send,
+    f_recv,
+    local_sem,
+):
     z, x, c = lax.axis_index("z"), lax.axis_index("x"), lax.axis_index("c")
+    y = lax.axis_index("y")
+    zz = lax.rem(z, 2)
+    rels = [(dz, dc) for dz in range(planes) for dc in range(2)]
+
+    def at(dz, dc):
+        return lax.rem(z + dz + planes, planes), lax.rem(c + dc + 2, 2)
+
+    def device(dz, dc):
+        there_z, there_c = at(dz, dc)
+        return (there_z, x, there_c, y)
+
+    x_mate = (z, 1 - x, c, y)
+    y_mate = (z, x, c, 1 - y)
+    c_mate = (z, x, 1 - c, y)
+    z_mate = (z + 1 - 2 * zz, x, c, y)
+
+    barrier = pltpu.get_barrier_semaphore()
+    peers = [device(*rel) for rel in rels[1:]] + [x_mate, y_mate]
+    for peer in peers:
+        pl.semaphore_signal(barrier, inc=1, device_id=peer, device_id_type=pl.DeviceIdType.MESH)
+    pl.semaphore_wait(barrier, len(peers))
+
+    def remote(src, dst, send, recv, to):
+        return pltpu.make_async_remote_copy(
+            src_ref=src,
+            dst_ref=dst,
+            send_sem=send,
+            recv_sem=recv,
+            device_id=to,
+            device_id_type=pl.DeviceIdType.MESH,
+        )
+
+    kv_cols = wk_ref.shape[1] // 4
+    q_cols = wq_ref.shape[1] // 4
+    weights = (
+        (wk_ref, kv_all, 0, kv_cols),
+        (wv_ref, kv_all, kv_cols, kv_cols),
+        (wq_ref, q_all, 0, q_cols),
+        (wo_ref, o_ref, 0, q_cols),
+    )
+
+    def slot(t, dz, dc, side):
+        there_z, there_c = at(-dz, -dc)
+        _, buf, low, cols = weights[t]
+        return buf.at[(there_z * 2 + side) * 2 + there_c, :, pl.ds(low, cols)]
+
+    def columns(t, dz, dc):
+        there_z, there_c = at(dz, dc)
+        ref, _, _, cols = weights[t]
+        first = pl.multiple_of((lax.rem(there_z, 2) * 2 + there_c) * cols, cols)
+        return ref.at[:, pl.ds(first, cols)]
+
+    def send(t, i):
+        return remote(
+            columns(t, *rels[i]), slot(t, 0, 0, x), w_send.at[t, i], w_recv.at[t, i], device(*rels[i])
+        )
+
+    def arrived(t, i):
+        here = slot(t, *rels[i], x)
+        return remote(here, here, w_send.at[t, i], w_recv.at[t, i], device(*rels[i]))
+
+    def forward(t, i):
+        here = slot(t, *rels[i], x)
+        source = columns(t, 0, 0) if i == 0 else here
+        return remote(source, here, f_send.at[t, i], f_recv.at[t, i], x_mate)
+
+    def forwarded(t, i):
+        here = slot(t, *rels[i], 1 - x)
+        return remote(here, here, f_send.at[t, i], f_recv.at[t, i], x_mate)
+
+    chunks = x_ref.shape[0]
+
+    def x_slot(row, core, half):
+        return x_all.at[pl.ds(half * chunks, chunks), row * 2 + core]
+
+    def x_copy(i, source, row, half, to):
+        return remote(source, x_slot(row, c, half), x_send.at[i], x_recv.at[i], to)
+
+    def x_arrived(i, row, core, half):
+        here = x_slot(row, core, half)
+        return remote(here, here, x_send.at[i], x_recv.at[i], z_mate)
+
+    def own(t):
+        return pltpu.make_async_copy(columns(t, 0, 0), slot(t, 0, 0, x), local_sem.at[t])
+
+    own_x = pltpu.make_async_copy(x_ref, x_slot(zz, c, y), local_sem.at[4])
+    x_copies = [
+        x_copy(0, x_ref, zz, y, z_mate),
+        x_copy(1, x_ref, zz, y, y_mate),
+        x_copy(2, x_ref, zz, y, c_mate),
+    ]
+    for copy in x_copies:
+        copy.start()
+    own_x.start()
+    for t in (0, 1, 2, 3):
+        own(t).start()
+
+    def send_all(t):
+        for i in range(1, len(rels)):
+            send(t, i).start()
+        forward(t, 0).start()
+
+    def forward_all(t):
+        for i in range(1, len(rels)):
+            arrived(t, i).wait_recv()
+            forward(t, i).start()
+
+    send_all(0)
+    send_all(1)
+    x_arrived(0, 1 - zz, c, y).wait_recv()
+    x_copies.append(x_copy(3, x_slot(1 - zz, c, y), 1 - zz, y, y_mate))
+    x_copies.append(x_copy(4, x_slot(1 - zz, c, y), 1 - zz, y, c_mate))
+    for copy in x_copies[3:]:
+        copy.start()
+    send_all(2)
+    x_arrived(1, zz, c, 1 - y).wait_recv()
+    x_copies.append(x_copy(5, x_slot(zz, c, 1 - y), zz, 1 - y, c_mate))
+    x_copies[5].start()
+    forward_all(0)
+    forward_all(1)
+    x_arrived(3, 1 - zz, c, 1 - y).wait_recv()
+    x_copies.append(x_copy(6, x_slot(1 - zz, c, 1 - y), 1 - zz, 1 - y, c_mate))
+    x_copies[6].start()
+    send_all(3)
+    forward_all(2)
+
+    x_arrived(2, zz, 1 - c, y).wait_recv()
+    x_arrived(4, 1 - zz, 1 - c, y).wait_recv()
+    x_arrived(5, zz, 1 - c, 1 - y).wait_recv()
+    x_arrived(6, 1 - zz, 1 - c, 1 - y).wait_recv()
+    own_x.wait()
+
+    def multiply(weight, out_ref):
+        blocks, tok = x_all.shape[1], x_all.shape[2]
+        out_ref[...] = jnp.zeros_like(out_ref)
+
+        def one(step, carry):
+            j, k = step // blocks, step % blocks
+            rows = pl.ds(pl.multiple_of(k * tok, tok), tok)
+            out_ref[rows, :] += jnp.dot(
+                x_all[j, k], weight[j], preferred_element_type=jnp.float32
+            )
+            return carry
+
+        lax.fori_loop(0, x_all.shape[0] * blocks, one, 0)
+
+    for t in (0, 1):
+        own(t).wait()
+        for i in range(len(rels)):
+            forwarded(t, i).wait_recv()
+    multiply(kv_all, kv_ref)
+    forward_all(3)
+    own(2).wait()
+    for i in range(len(rels)):
+        forwarded(2, i).wait_recv()
+    multiply(q_all, q_ref)
+    own(3).wait()
+    for i in range(len(rels)):
+        forwarded(3, i).wait_recv()
+    for copy in x_copies:
+        copy.wait_send()
+    for t in range(4):
+        for i in range(len(rels)):
+            if i > 0:
+                send(t, i).wait_send()
+            forward(t, i).wait_send()
+
+
+def gathered_products(normed, key_weight, value_weight, w_query, w_out):
+    tok, half_width = normed.shape
+    rows = key_weight.shape[0]
     planes = lax.axis_size("z")
-    own = jnp.moveaxis(pick(weight, c, 2), 1, 0)
-    other = swap(jnp.moveaxis(pick(weight, 1 - c, 2), 1, 0), "c")
-    block = in_order(c, own, other, axis=1).reshape(2, 2 * rows, cols)
-    pieces = [(z, pick(block, z % 2, 0))]
-    for distance in range(1, planes):
-        piece = pick(block, (z + distance) % 2, 0)
-        pieces.append(((z - distance + planes) % planes, shift(piece, "z", distance)))
-    whole = jnp.zeros((planes, 2, 2 * rows, cols), weight.dtype)
-    for place, piece in pieces:
-        across = swap(piece, "x")
-        whole = lax.dynamic_update_slice(whole, piece[None, None], (place, x, 0, 0))
-        whole = lax.dynamic_update_slice(whole, across[None, None], (place, 1 - x, 0, 0))
-    return whole.reshape(planes * 4 * rows, cols)
+    kv_cols, q_cols = key_weight.shape[1] // 2, w_query.shape[1] // 4
+    places = planes * 4
+    chunks = half_width // rows
+    split = jnp.transpose(normed.reshape(tok, chunks, rows), (1, 0, 2))
+    any_space = pl.BlockSpec(memory_space=pl.ANY)
+    vmem_space = pl.BlockSpec(memory_space=pltpu.VMEM)
+    dma = pltpu.SemaphoreType.DMA
+    kv_raw, q_raw, o_all = pl.pallas_call(
+        functools.partial(gather_kernel, planes),
+        out_shape=(
+            jax.ShapeDtypeStruct((4 * tok, kv_cols), jnp.float32),
+            jax.ShapeDtypeStruct((4 * tok, q_cols), jnp.float32),
+            jax.ShapeDtypeStruct((places, rows, q_cols), jnp.bfloat16),
+        ),
+        in_specs=[any_space] * 5,
+        out_specs=(vmem_space, vmem_space, any_space),
+        scratch_shapes=[
+            pltpu.VMEM((places, 4, tok, rows), jnp.bfloat16),
+            pltpu.VMEM((places, rows, kv_cols), jnp.bfloat16),
+            pltpu.VMEM((places, rows, q_cols), jnp.bfloat16),
+            dma((7,)),
+            dma((7,)),
+            dma((4, places // 2)),
+            dma((4, places // 2)),
+            dma((4, places // 2)),
+            dma((4, places // 2)),
+            dma((5,)),
+        ],
+        compiler_params=pltpu.CompilerParams(
+            collective_id=0, has_side_effects=True, vmem_limit_bytes=44 << 20
+        ),
+    )(split, key_weight, value_weight, w_query, w_out)
+    return kv_raw, q_raw, o_all.reshape(places * rows, q_cols)
 
 
 def rearranged(
@@ -191,7 +405,6 @@
     z, x, c = lax.axis_index("z"), lax.axis_index("x"), lax.axis_index("c")
     y = lax.axis_index("y")
     pair, zz = z // 2, z % 2
-    rows = w_query.shape[0]
     kv_cols = key_weight.shape[1] // 4
     q_cols = w_query.shape[1] // 4
     kv_heads = kv_cols // head_dim
@@ -204,29 +417,14 @@
     squares = squares + swap(squares, "y")
     gain_in = lax.dynamic_slice_in_dim(input_gain, y * half_width, half_width, 0)
     normed = (stream * lax.rsqrt(squares / full_width + epsilon) * gain_in).astype(jnp.bfloat16)
-    normed = in_order(zz, normed, swap(normed, "z"))
-    other = swap(normed, "y")
-    normed = jnp.concatenate(
-        [jnp.where(y == 0, normed, other), jnp.where(y == 0, other, normed)], axis=-1
-    )
-    normed = in_order(c, normed, swap(normed, "c"), axis=1).reshape(2 * run, full_width)
-
-    kv_weight = jnp.concatenate(
-        [
-            key_weight.reshape(rows, 2, 2, kv_cols),
-            value_weight.reshape(rows, 2, 2, kv_cols),
-        ],
-        axis=-1,
-    )
-    kv_all = spread(kv_weight)
-    q_all = spread(w_query.reshape(rows, 2, 2, q_cols))
-    o_all = spread(w_out.T.reshape(rows, 2, 2, q_cols))
+    kv_raw, q_raw, o_all = gathered_products(
+        normed, key_weight, value_weight, w_query, w_out.T
+    )
 
     def places_of(i):
         return lax.dynamic_slice_in_dim(positions, (4 * pair + 2 * i + x) * run, run, 0)
 
     places = jnp.concatenate([places_of(0), places_of(1)])
-    kv_raw = jnp.dot(normed, kv_all, preferred_element_type=jnp.float32)
     keys = rotary(
         norm_scale(kv_raw[:, :kv_cols].reshape(2 * run, kv_heads, head_dim), key_gain), places
     ).reshape(2 * run, kv_cols)
@@ -242,7 +440,6 @@
     key_index = (4 * pair - 2) * run + jnp.arange(6 * run, dtype=jnp.int32)
     key_places = jnp.where(key_index >= 0, key_places, jnp.int32(1 << 30))
 
-    q_raw = jnp.dot(normed, q_all, preferred_element_type=jnp.float32)
     queries = rotary(
         norm_scale(q_raw.reshape(2 * run, kv_heads * group, head_dim), query_gain), places
     ).astype(jnp.bfloat16)

time: 522 us -> 477 us (0.914)
  Pallas kernels: 0 us -> 259 us
  waiting for transfers between devices: 177 us -> 41.7 us
  starting transfers between devices: 122 us -> 12.5 us
  local copies, waits for them, and re-layouts: 120 us -> 90.1 us
  matrix products: 42.4 us -> 23.4 us
  other arithmetic: 49.6 us -> 40.4 us
    pallas_call x0 -> x1, Pallas kernels: none -> 259 us  [gathered_products(): pl.pallas_call(functools.partial(gather_kernel, planes), out_shape=(jax.S...]
    ppermute x28 -> x10, waiting for transfers between devices: 145 us -> 41.7 us  [swap(): return lax.ppermute(block, axis, [(i, i ^ 1) for i in range(size)])]
    ppermute x9 -> x0, starting transfers between devices: 85.7 us -> none  [shift(): lax.ppermute(block, axis, [(i, (i + distance) % size) for i in range(size)])]
    ppermute x9 -> x0, waiting for transfers between devices: 31.9 us -> none  [shift(): lax.ppermute(block, axis, [(i, (i + distance) % size) for i in range(size)])]
    dynamic_update_slice x24 -> x0, local copies, waits for them, and re-layouts: 22.5 us -> none  [the longest x12 12.2 us: spread(): lax.dynamic_update_slice(whole, across[None, None], (place, 1 - x, 0, 0))]
    ppermute x28 -> x10, starting transfers between devices: 33.1 us -> 10.9 us  [swap(): return lax.ppermute(block, axis, [(i, i ^ 1) for i in range(size)])]
    dot_general x2 -> x0, matrix products: 20.5 us -> none  [the longest x1 10.5 us: rearranged(): q_raw = jnp.dot(normed, q_all, preferred_element_type=jnp.float32)]
    another operation x10 -> x1, other arithmetic: 14 us -> 0.29 us  [in_order(): jnp.stack([jnp.where(at == 0, own, other), jnp.where(at == 0, other, own)...]
  transfers between devices with their start and end apart: 38 -> 11, of which waited for: 18 -> 5; matrix products, arithmetic and copies ran while one was open for 29% -> 19% of each run, Pallas kernels for 0% -> 0%
where the time goes in v2:
time: 477 us; the launch traced here: 468 us
  Pallas kernels  259 us (54%)
  local copies, waits for them, and re-layouts  90.1 us (19%)
  waiting for transfers between devices  41.7 us (9%)
  other arithmetic  40.4 us (8%)
  matrix products  23.4 us (5%)
  starting transfers between devices  12.5 us (3%)
    pallas_call x1, Pallas kernels, gathered_products(): pl.pallas_call(functools.partial(gather_kernel, planes), out_shape=(jax.S...  259 us
    ppermute x10, waiting for transfers between devices, swap(): return lax.ppermute(block, axis, [(i, i ^ 1) for i in range(size)])  41.7 us
    dynamic_slice x6, local copies, waits for them, and re-layouts, pick(): return lax.dynamic_index_in_dim(block, index, axis, keepdims=False)  25.5 us
    unnamed x60, local copies, waits for them, and re-layouts  22.9 us
    reshape x2, local copies, waits for them, and re-layouts, rearranged(): part = part.reshape(2, tok, 2, width)  15.6 us
    add x2, other arithmetic, rearranged(): pick(part, c, 1)  12.2 us
    ppermute x10, starting transfers between devices, swap(): return lax.ppermute(block, axis, [(i, i ^ 1) for i in range(size)])  10.9 us
  transfers between devices with their start and end apart: 11, of which 5 were waited for; matrix products, arithmetic and copies ran while one was open for 19% of the time, Pallas kernels for 0%

profile of v2, /device:TPU:0, one launch (start us, length us, event | category | flops | bytes accessed | tf_op | source)
XLA Modules:
  0.0 468.2 jit_solution(8222290165630807557)
XLA Ops:
  2.2 3.0 collective-permute-start
  5.4 3.0 multiply_cosine_fusion
  8.4 2.7 fusion.14
  18.1 259.0 %shard_map.100 = (f32[1024,512]{1,0:T(8,128)S(1)}, f32[1024,512]{1,0:T(8,128)S(1)}, bf16[16,336,512]{2,1,0:T(8,128)(2,1)}) custom-call(bf16[8,256,336]{2,1,0:T(8,128)(2,1)S(1)} %bitcast.124, bf16[336,1024]{1,0:T(8,128)(2,1)S(1)} %copy-done.4, bf16[336,1024]{1,0:T(8,128)(2,1)S(1)} %copy-done.5, bf16[336,2048]{1,0:T(8,128)(2,1)S(1)} %copy-done.2, ...), custom_call_target="tpu_custom_call" | custom-call | tf_op jit(solution)/shard_map/pallas_call | solution.py:363
  285.2 2.4 multiply_multiply_fusion.1
  298.2 3.5 slice.70
  303.5 2.4 multiply_multiply_fusion
  312.9 12.3 %collective-permute-done.2 = bf16[512,512]{1,0:T(8,128)(2,1)S(1)} collective-permute-done((bf16[512,512]{1,0:T(8,128)(2,1)S(1)}, bf16[512,512]{1,0:T(8,128)(2,1)S(1)}, u32[]{:S(2)}, u32[]{:S(2)}) %collective-permute-start.2) | collective-permute-done | bytes 524320 | tf_op jit(solution)/shard_map/ppermute | solution.py:144
  328.9 4.6 fusion.2
  333.6 2.7 divide_convert_fusion
  336.3 3.9 fusion
  340.2 2.8 divide_convert_fusion.1
  343.9 5.0 %fusion.44 = f32[2,2,256,2560]{3,2,1,0:T(8,128)S(1)} fusion(bf16[2,2,256,512]{3,2,1,0:T(8,128)(2,1)S(1)} %bitcast.139, bf16[2560,512,1,1]{1,0,3,2:T(8,128)(2,1)} %bitcast.135), kind=kOutput, calls=%fused_computation.97 | convolution fusion | flops 2684354560 | bytes 14155776 | tf_op jit(solution)/shard_map/dot_general | solution.py:480
  350.8 3.5 copy-done.10
  354.2 4.4 fusion.43
  358.7 4.3 copy-done.9
  364.8 5.7 %bitcast_add_fusion.1 = f32[2,256,2560]{2,1,0:T(8,128)} fusion(bf16[2,256,2560]{2,1,0:T(8,128)(2,1)S(1)} %collective-permute-done.7, f32[2,2,256,2560]{3,2,1,0:T(8,128)} %copy-done.10, s32[]{:T(128)S(6)} %select_n.114), kind=kLoop, calls=%fused_computation.16 | loop fusion | flops 2621440 | bytes 13107204 | tf_op jit(solution)/shard_map/add | solution.py:487
  370.5 7.6 %reshape.371 = f32[2,256,2,1280]{3,2,1,0:T(2,128)} reshape(f32[2,256,2560]{2,1,0:T(8,128)} %bitcast_add_fusion.1) | data formatting | bytes 10485760 | tf_op jit(solution)/shard_map/reshape | solution.py:490
  378.1 4.8 %constant_dynamic-slice_fusion = bf16[2,256,1,1280]{3,2,1,0:T(2,128)(2,1)S(1)} fusion(f32[2,256,2,1280]{3,2,1,0:T(2,128)} %reshape.371, s32[]{:T(128)S(6)} %select_n.120), kind=kLoop, calls=%fused_computation.80 | loop fusion | bytes 2621444 | tf_op jit(solution)/shard_map/jit(dynamic_index_in_dim)/dynamic_slice | solution.py:153
  382.9 3.8 copy.97
  387.2 6.5 %bitcast_add_fusion = f32[2,256,2816]{2,1,0:T(8,128)} fusion(bf16[2,256,2816]{2,1,0:T(8,128)(2,1)} %collective-permute-done.4, f32[2,2,256,2816]{3,2,1,0:T(8,128)} %copy-done.9, s32[]{:T(128)S(6)} %select_n.114), kind=kLoop, calls=%fused_computation.14 | loop fusion | flops 2883584 | bytes 14417924 | tf_op jit(solution)/shard_map/add | solution.py:487
  393.7 8.1 %reshape.369 = f32[2,256,2,1408]{3,2,1,0:T(2,128)} reshape(f32[2,256,2816]{2,1,0:T(8,128)} %bitcast_add_fusion) | data formatting | bytes 11534336 | tf_op jit(solution)/shard_map/reshape | solution.py:490
  401.8 2.8 constant_dynamic-slice_fusion.2
  404.6 3.3 copy.96
  408.0 5.2 %constant_dynamic-slice_fusion.1 = f32[2,256,1,1280]{3,2,1,0:T(1,128)S(1)} fusion(f32[2,256,2,1280]{3,2,1,0:T(2,128)} %reshape.371, s32[]{:T(128)S(6)} %select_n.119), kind=kLoop, calls=%fused_computation.81 | loop fusion | bytes 5242884 | tf_op jit(solution)/shard_map/jit(dynamic_index_in_dim)/dynamic_slice | solution.py:153
  413.1 4.1 copy.81
  417.2 4.4 constant_dynamic-slice_fusion.3
  421.7 4.1 copy.79
  425.8 2.4 bitcast_add_fusion.3
  430.4 12.3 %collective-permute-done.5 = bf16[256,2,1408]{0,2,1:T(8,128)(2,1)} collective-permute-done((bf16[256,2,1408]{0,2,1:T(8,128)(2,1)}, bf16[256,2,1408]{0,2,1:T(8,128)(2,1)}, u32[]{:S(2)}, u32[]{:S(2)}) %collective-permute-start.5) | collective-permute-done | bytes 1441824 | tf_op jit(solution)/shard_map/ppermute | solution.py:144
  446.0 9.9 %collective-permute-done.9 = bf16[256,1280]{0,1:T(8,128)(2,1)S(1)} collective-permute-done((bf16[256,1280]{0,1:T(8,128)(2,1)S(1)}, bf16[256,1280]{0,1:T(8,128)(2,1)S(1)}, u32[]{:S(2)}, u32[]{:S(2)}) %collective-permute-start.9) | collective-permute-done | bytes 655392 | tf_op jit(solution)/shard_map/ppermute | solution.py:144
  456.1 5.2 %collective-permute-done.6 = bf16[256,1408]{0,1:T(8,128)(2,1)S(1)} collective-permute-done((bf16[256,1408]{0,1:T(8,128)(2,1)S(1)}, bf16[256,1408]{0,1:T(8,128)(2,1)S(1)}, u32[]{:S(2)}, u32[]{:S(2)}) %collective-permute-start.6) | collective-permute-done | bytes 720928 | tf_op jit(solution)/shard_map/ppermute | solution.py:144
  (123 shorter events, 57.4 us)
Async XLA Ops:
  0.0 5.3 %copy-start.21 = (s32[4096]{0:T(1024)S(1)}, s32[4096]{0:T(1024)}, u32[]{:S(2)}) copy-start(s32[4096]{0:T(1024)} %param.19) | copy-start | bytes 49156
  1.8 10.9 %copy-start.6 = (bf16[256,2688]{0,1:T(8,128)(2,1)}, bf16[256,2688]{0,1:T(8,128)(2,1)S(1)}, u32[]{:S(2)}) copy-start(bf16[256,2688]{0,1:T(8,128)(2,1)S(1)} %copy.61) | copy-start | bytes 4128772
  1.8 9.3 %copy-start.22 = (f32[5376]{0:T(1024)S(1)}, f32[5376]{0:T(1024)}, u32[]{:S(2)}) copy-start(f32[5376]{0:T(1024)} %param.11) | copy-start | bytes 64516
  2.2 8.9 %collective-permute-start = (f32[256,1]{0,1:T(1,128)S(1)}, f32[256,1]{0,1:T(1,128)S(1)}, u32[]{:S(2)}, u32[]{:S(2)}) collective-permute-start(f32[256,1]{0,1:T(1,128)S(1)} %bitcast.154), channel_id=1, source_target_pairs={{0,1},{1,0},{2,3},{3,2},{4,5},{5,4},{6,7},{7,6},{8,9},{9,8},{10,11... | collective-permute-start | bytes 3080 | tf_op jit(solution)/shard_map/ppermute | solution.py:144
  11.2 3.4 copy-start.2
  282.2 3.0 copy-start.25
  284.0 3.7 copy-start.11
  289.4 5.7 %copy-start.8 = (f32[1024,4,128]{2,1,0:T(4,128)S(1)}, f32[1024,4,128]{2,1,0:T(4,128)}, u32[]{:S(2)}) copy-start(f32[1024,4,128]{2,1,0:T(4,128)} %reshape.363) | copy-start | bytes 6291460
  293.8 2.4 copy-start.12
  293.8 4.1 copy-start.14
  295.0 6.7 %slice-start = ((s8[5505024]{0:T(1024)(128)(4,1)}), s8[4194304]{0:T(1024)(128)(4,1)S(1)}, s32[]{:S(2)}) async-start(s8[5505024]{0:T(1024)(128)(4,1)} %bitcast.128), calls=%async_computation | async-start | bytes 8388608
  296.3 9.7 %collective-permute-start.1 = (bf16[512,512]{1,0:T(8,128)(2,1)S(1)}, bf16[512,512]{1,0:T(8,128)(2,1)S(1)}, u32[]{:S(2)}, u32[]{:S(2)}) collective-permute-start(bf16[512,512]{1,0:T(8,128)(2,1)S(1)} %pad_maximum_fusion.7), channel_id=1, source_target_pairs={{0,16},{8,24},{1,17},{9,25},{2,18},{10,26},{3,19},{11,27},{4,20},{... | collective-permute-start | bytes 1572872 | tf_op jit(solution)/shard_map/ppermute | solution.py:22
  297.9 3.8 slice-start.1
  298.1 27.1 %collective-permute-start.3 = (bf16[2,512,512]{2,1,0:T(8,128)(2,1)S(1)}, bf16[2,512,512]{2,1,0:T(8,128)(2,1)S(1)}, u32[]{:S(2)}, u32[]{:S(2)}) collective-permute-start(bf16[2,512,512]{2,1,0:T(8,128)(2,1)S(1)} %get-tuple-element.24), channel_id=1, source_target_pairs={{0,4},{4,0},{1,5},{5,1},{2,6},{6,2},{3,7},{7,3},{8,12},{12,8},{9,1... | collective-permute-start | bytes 3145736 | tf_op jit(solution)/shard_map/ppermute | solution.py:144
  305.9 19.3 %collective-permute-start.2 = (bf16[512,512]{1,0:T(8,128)(2,1)S(1)}, bf16[512,512]{1,0:T(8,128)(2,1)S(1)}, u32[]{:S(2)}, u32[]{:S(2)}) collective-permute-start(bf16[512,512]{1,0:T(8,128)(2,1)S(1)} %collective-permute-done.1), channel_id=1, source_target_pairs={{0,4},{4,0},{1,5},{5,1},{2,6},{6,2},{3,7},{7,3},{8,12},{12,8},{9,1... | collective-permute-start | bytes 1572872 | tf_op jit(solution)/shard_map/ppermute | solution.py:144
  328.9 4.6 copy-start.19
  333.5 2.8 copy-start.16
  333.6 2.8 copy-start.18
  333.6 2.8 copy-start.20
  343.9 5.0 %copy-start.15 = (bf16[1024,512]{1,0:T(8,128)(2,1)}, bf16[1024,512]{1,0:T(8,128)(2,1)S(1)}, u32[]{:S(2)}) copy-start(bf16[1024,512]{1,0:T(8,128)(2,1)S(1)} %copy.78) | copy-start | bytes 3145732
  348.9 5.3 %copy-start.10 = (f32[2,2,256,2560]{3,2,1,0:T(8,128)}, f32[2,2,256,2560]{3,2,1,0:T(8,128)S(1)}, u32[]{:S(2)}) copy-start(f32[2,2,256,2560]{3,2,1,0:T(8,128)S(1)} %fusion.44) | copy-start | bytes 31457284
  348.9 5.3 %copy-start.13 = (bf16[2,1408,512]{2,1,0:T(8,128)(2,1)S(1)}, bf16[2,1408,512]{2,1,0:T(8,128)(2,1)}, u32[]{:S(2)}) copy-start(bf16[2,1408,512]{2,1,0:T(8,128)(2,1)} %slice.69) | copy-start | bytes 8650756
  350.7 14.0 %collective-permute-start.7 = (bf16[2,256,2560]{2,1,0:T(8,128)(2,1)}, bf16[2,256,2560]{2,1,0:T(8,128)(2,1)S(1)}, u32[]{:S(2)}, u32[]{:S(2)}) collective-permute-start(bf16[2,256,2560]{2,1,0:T(8,128)(2,1)} %fusion.21), channel_id=1, source_target_pairs={{0,2},{2,0},{1,3},{3,1},{4,6},{6,4},{5,7},{7,5},{8,10},{10,8},{9,1... | collective-permute-start | bytes 7864328 | tf_op jit(solution)/shard_map/ppermute | solution.py:144
  358.7 4.3 copy-start.9
  364.8 22.5 %collective-permute-start.4 = (bf16[2,256,2816]{2,1,0:T(8,128)(2,1)}, bf16[2,256,2816]{2,1,0:T(8,128)(2,1)}, u32[]{:S(2)}, u32[]{:S(2)}) collective-permute-start(bf16[2,256,2816]{2,1,0:T(8,128)(2,1)} %fusion.16), channel_id=1, source_target_pairs={{0,2},{2,0},{1,3},{3,1},{4,6},{6,4},{5,7},{7,5},{8,10},{10,8},{9,1... | collective-permute-start | bytes 8650760 | tf_op jit(solution)/shard_map/ppermute | solution.py:144
  386.7 39.1 %collective-permute-start.8 = (bf16[2,256,1280]{1,2,0:T(8,128)(2,1)}, bf16[2,256,1280]{1,2,0:T(8,128)(2,1)}, u32[]{:S(2)}, u32[]{:S(2)}) collective-permute-start(bf16[2,256,1280]{1,2,0:T(8,128)(2,1)} %bitcast.137), channel_id=1, source_target_pairs={{0,1},{1,0},{2,3},{3,2},{4,5},{5,4},{6,7},{7,6},{8,9},{9,8},{10,11... | collective-permute-start | bytes 3932168 | tf_op jit(solution)/shard_map/ppermute | solution.py:144
  407.9 34.7 %collective-permute-start.5 = (bf16[256,2,1408]{0,2,1:T(8,128)(2,1)}, bf16[256,2,1408]{0,2,1:T(8,128)(2,1)}, u32[]{:S(2)}, u32[]{:S(2)}) collective-permute-start(bf16[256,2,1408]{0,2,1:T(8,128)(2,1)} %bitcast.111), channel_id=1, source_target_pairs={{0,8},{8,0},{16,24},{24,16},{1,9},{9,1},{17,25},{25,17},{2,10},{10... | collective-permute-start | bytes 4325384 | tf_op jit(solution)/shard_map/ppermute | solution.py:144
  428.3 27.6 %collective-permute-start.9 = (bf16[256,1280]{0,1:T(8,128)(2,1)S(1)}, bf16[256,1280]{0,1:T(8,128)(2,1)S(1)}, u32[]{:S(2)}, u32[]{:S(2)}) collective-permute-start(bf16[256,1280]{0,1:T(8,128)(2,1)S(1)} %fusion.33), channel_id=1, source_target_pairs={{0,8},{8,0},{16,24},{24,16},{1,9},{9,1},{17,25},{25,17},{2,10},{10... | collective-permute-start | bytes 1966088 | tf_op jit(solution)/shard_map/ppermute | solution.py:144
  444.4 16.8 %collective-permute-start.6 = (bf16[256,1408]{0,1:T(8,128)(2,1)S(1)}, bf16[256,1408]{0,1:T(8,128)(2,1)S(1)}, u32[]{:S(2)}, u32[]{:S(2)}) collective-permute-start(bf16[256,1408]{0,1:T(8,128)(2,1)S(1)} %fusion.32), channel_id=1, source_target_pairs={{0,1},{1,0},{2,3},{3,2},{4,5},{5,4},{6,7},{7,6},{8,9},{9,8},{10,11... | collective-permute-start | bytes 2162696 | tf_op jit(solution)/shard_map/ppermute | solution.py:144
  456.1 7.3 %copy-start.23 = (f32[5376]{0:T(1024)S(1)}, f32[5376]{0:T(1024)}, u32[]{:S(2)}) copy-start(f32[5376]{0:T(1024)} %param.18) | copy-start | bytes 64516
  456.1 9.3 %copy-start.7 = (bf16[256,2688]{0,1:T(8,128)(2,1)S(1)}, bf16[256,2688]{0,1:T(8,128)(2,1)}, u32[]{:S(2)}) copy-start(bf16[256,2688]{0,1:T(8,128)(2,1)} %copy-done.6) | copy-start | bytes 4128772
  461.8 3.6 collective-permute-start.10
  (7 other events, 10.4 us)

commit v3 on v2

--- a/solution.py
+++ b/solution.py
@@ -225,6 +225,8 @@
     def slot(t, dz, dc, side):
         there_z, there_c = at(-dz, -dc)
         _, buf, low, cols = weights[t]
+        if t == 3:
+            there_z = lax.rem(there_z + y * (planes // 2), planes)
         return buf.at[(there_z * 2 + side) * 2 + there_c, :, pl.ds(low, cols)]
 
     def columns(t, dz, dc):
@@ -278,34 +280,40 @@
     for t in (0, 1, 2, 3):
         own(t).start()
 
-    def send_all(t):
-        for i in range(1, len(rels)):
-            send(t, i).start()
-        forward(t, 0).start()
-
-    def forward_all(t):
-        for i in range(1, len(rels)):
-            arrived(t, i).wait_recv()
-            forward(t, i).start()
-
-    send_all(0)
-    send_all(1)
+    order = [1] + list(range(4, 6)) + list(range(2, 4)) + list(range(6, len(rels)))
+    items = [(t, i) for t in range(4) for i in order]
+    window = len(order) + 1
+
+    def start_item(n):
+        if n < len(items):
+            send(*items[n]).start()
+            if items[n][1] == order[0]:
+                forward(items[n][0], 0).start()
+
+    def roll(first, last):
+        for n in range(first, last):
+            arrived(*items[n]).wait_recv()
+            start_item(n + window)
+            forward(*items[n]).start()
+
+    for n in range(window):
+        start_item(n)
+    roll(0, 2)
     x_arrived(0, 1 - zz, c, y).wait_recv()
     x_copies.append(x_copy(3, x_slot(1 - zz, c, y), 1 - zz, y, y_mate))
     x_copies.append(x_copy(4, x_slot(1 - zz, c, y), 1 - zz, y, c_mate))
     for copy in x_copies[3:]:
         copy.start()
-    send_all(2)
+    roll(2, 7)
     x_arrived(1, zz, c, 1 - y).wait_recv()
     x_copies.append(x_copy(5, x_slot(zz, c, 1 - y), zz, 1 - y, c_mate))
     x_copies[5].start()
-    forward_all(0)
-    forward_all(1)
+    per = len(order)
+    roll(7, 2 * per)
     x_arrived(3, 1 - zz, c, 1 - y).wait_recv()
     x_copies.append(x_copy(6, x_slot(1 - zz, c, 1 - y), 1 - zz, 1 - y, c_mate))
     x_copies[6].start()
-    send_all(3)
-    forward_all(2)
+    roll(2 * per, 3 * per)
 
     x_arrived(2, zz, 1 - c, y).wait_recv()
     x_arrived(4, 1 - zz, 1 - c, y).wait_recv()
@@ -332,7 +340,7 @@
         for i in range(len(rels)):
             forwarded(t, i).wait_recv()
     multiply(kv_all, kv_ref)
-    forward_all(3)
+    roll(3 * per, 4 * per)
     own(2).wait()
     for i in range(len(rels)):
         forwarded(2, i).wait_recv()
@@ -470,31 +478,30 @@
         merged = summed / jnp.transpose(total, (2, 0, 1))[..., None]
         return merged.astype(jnp.bfloat16).reshape(run, q_cols)
 
-    attended = jnp.concatenate([attend(0), attend(1)])
-
-    cut = (half_width // 2 + 127) // 128 * 128
-    o_halves = o_all.reshape(2, half_width, q_cols)
-    sums = []
-    for low, high, z_first in ((0, cut, True), (cut, half_width, False)):
-        width = high - low
-        part = lax.dot_general(
-            attended,
-            o_halves[:, low:high].reshape(2 * width, q_cols),
-            (((1,), (1,)), ((), ())),
-            preferred_element_type=jnp.float32,
-        )
-        part = part.reshape(2, 2, tok, 2 * width)
-        part = pick(part, c, 1) + swap(pick(part, 1 - c, 1).astype(jnp.bfloat16), "c").astype(
-            jnp.float32
-        )
-        part = part.reshape(2, tok, 2, width)
-        for axis in ("z", "y") if z_first else ("y", "z"):
-            at, dim = (zz, 0) if axis == "z" else (y, part.ndim - 2)
-            part = pick(part, at, dim) + swap(
-                pick(part, 1 - at, dim).astype(jnp.bfloat16), axis
-            ).astype(jnp.float32)
-        sums.append(part)
-    attn_sum = jnp.concatenate(sums, axis=1)
+    attended = jnp.stack([attend(0), attend(1)]).reshape(2, 2, tok, q_cols)
+
+    def project(block):
+        return lax.dot_general(
+            block, o_all, (((1,), (1,)), ((), ())), preferred_element_type=jnp.float32
+        )
+
+    def exchange(block, axis):
+        return swap(block.astype(jnp.bfloat16), axis).astype(jnp.float32)
+
+    def core_sum(block):
+        return exchange(project(pick(block, 1 - c, 0)), "c") + project(pick(block, c, 0))
+
+    half_tok = tok // 2
+    away = core_sum(pick(attended, 1 - zz, 0))
+    home = core_sum(pick(attended, zz, 0))
+    first = exchange(away[:half_tok], "z")
+    away_cross = exchange(away[half_tok:, half_width:], "y")
+    home_cross = exchange(home[half_tok:, half_width:], "y")
+    upper = home[:half_tok] + first
+    lower = away[half_tok:, :half_width] + away_cross
+    upper_sum = upper[:, :half_width] + exchange(upper[:, half_width:], "y")
+    lower_sum = home[half_tok:, :half_width] + home_cross + exchange(lower, "z")
+    attn_sum = jnp.concatenate([upper_sum, lower_sum], axis=0)
     squares = jnp.sum(attn_sum * attn_sum, axis=1, keepdims=True)
     squares = squares + swap(squares, "y")
     gain_out = lax.dynamic_slice_in_dim(post_gain, y * half_width, half_width, 0)
@@ -505,7 +512,7 @@
 
 def solution(mesh):
     seq, tp = mesh.shape["seq"], mesh.shape["tp"]
-    if tp == 2 and seq % 8 == 0:
+    if tp == 2 and seq % 16 == 0:
         mesh = Mesh(mesh.devices.reshape(seq // 4, 2, 2, tp), ("z", "x", "c", "y"))
         seq_axes, tp_axes, body = ("z", "x", "c"), "y", rearranged
     else:

time: 477 us -> 410 us (0.86); the launches traced: 468 us -> 409 us
  local copies, waits for them, and re-layouts: 90.1 us -> 22.6 us
  starting transfers between devices: 12.5 us -> 49.9 us
  Pallas kernels: 259 us -> 226 us
  matrix products: 23.4 us -> 36.1 us
  other arithmetic: 40.4 us -> 32.1 us
    pallas_call x1, Pallas kernels: 259 us -> 226 us  [gathered_products(): pl.pallas_call(functools.partial(gather_kernel, planes), out_shape=(jax.S...]
    ppermute x10 -> x11, starting transfers between devices: 10.9 us -> 40.6 us  [swap(): return lax.ppermute(block, axis, [(i, i ^ 1) for i in range(size)])]
    dynamic_slice x6 -> x0, local copies, waits for them, and re-layouts: 25.5 us -> none  [pick(): return lax.dynamic_index_in_dim(block, index, axis, keepdims=False)]
    unnamed x60 -> x51, local copies, waits for them, and re-layouts: 22.9 us -> 5.01 us
    add x6 -> x3, other arithmetic: 16.5 us -> 0.59 us  [the longest x1 0.22 us: rearranged(): upper = home[:half_tok] + first]
    reshape x2 -> x0, local copies, waits for them, and re-layouts: 15.6 us -> none  [rearranged(): part = part.reshape(2, tok, 2, width)]
    dot_general x2 -> x4, matrix products: 9.44 us -> 20.2 us  [project(): lax.dot_general(block, o_all, (((1,), (1,)), ((), ())), preferred_element...]
    ppermute x1, starting transfers between devices: 1.63 us -> 9.29 us  [from_behind(): return lax.ppermute(block, axis, route)]
  transfers between devices with their start and end apart: 11 -> 12, of which waited for: 5 -> 6; matrix products, arithmetic and copies ran while one was open for 19% -> 9% of each run, Pallas kernels for 0% -> 0%
where the time goes in v3:
time: 410 us; the launch traced here: 409 us
  Pallas kernels  226 us (55%)
  starting transfers between devices  49.9 us (12%)
  waiting for transfers between devices  41.5 us (10%)
  matrix products  36.1 us (9%)
  other arithmetic  32.1 us (8%)
  local copies, waits for them, and re-layouts  22.6 us (6%)
    pallas_call x1, Pallas kernels, gathered_products(): pl.pallas_call(functools.partial(gather_kernel, planes), out_shape=(jax.S...  226 us
    ppermute x11, starting transfers between devices, swap(): return lax.ppermute(block, axis, [(i, i ^ 1) for i in range(size)])  40.6 us
    ppermute x11, waiting for transfers between devices, swap(): return lax.ppermute(block, axis, [(i, i ^ 1) for i in range(size)])  38.3 us
    dot_general x4, matrix products, project(): lax.dot_general(block, o_all, (((1,), (1,)), ((), ())), preferred_element...  20.2 us
    dot_general x2, matrix products, attend(): jnp.einsum('qkgd,skd->kgqs', queries[i], window_keys, preferred_element_t...  9.69 us
    ppermute x1, starting transfers between devices, from_behind(): return lax.ppermute(block, axis, route)  9.29 us
  transfers between devices with their start and end apart: 12, of which 6 were waited for; matrix products, arithmetic and copies ran while one was open for 9% of the time, Pallas kernels for 0%

profile of v3, /device:TPU:0, one launch (start us, length us, event | category | flops | bytes accessed | tf_op | source)
XLA Modules:
  0.0 409.2 jit_solution(5822605892258317159)
XLA Ops:
  0.0 1.8 fusion.16
  1.8 3.0 collective-permute-start
  5.6 3.0 multiply_cosine_fusion
  9.4 2.7 fusion.14
  14.2 1.8 copy.50
  19.5 226.4 %shard_map.100 = (f32[1024,512]{1,0:T(8,128)S(1)}, f32[1024,512]{1,0:T(8,128)S(1)}, bf16[16,336,512]{2,1,0:T(8,128)(2,1)}) custom-call(bf16[8,256,336]{2,1,0:T(8,128)(2,1)S(1)} %bitcast.111, bf16[336,1024]{1,0:T(8,128)(2,1)S(1)} %copy-done.4, bf16[336,1024]{1,0:T(8,128)(2,1)S(1)} %copy-done.5, bf16[336,2048]{1,0:T(8,128)(2,1)S(1)} %copy-done.2, ...), custom_call_target="tpu_custom_call" | custom-call | tf_op jit(solution)/shard_map/pallas_call | solution.py:371
  250.1 2.4 multiply_multiply_fusion.1
  252.5 1.7 multiply_subtract_fusion
  256.8 2.8 fusion.64
  261.6 9.3 %collective-permute-start.1 = (bf16[512,512]{1,0:T(8,128)(2,1)}, bf16[512,512]{1,0:T(8,128)(2,1)}, u32[]{:S(2)}, u32[]{:S(2)}) collective-permute-start(bf16[512,512]{1,0:T(8,128)(2,1)} %pad_maximum_fusion.6), channel_id=1, source_target_pairs={{0,16},{8,24},{1,17},{9,25},{2,18},{10,26},{3,19},{11,27},{4,20},{... | collective-permute-start | bytes 1572872 | tf_op jit(solution)/shard_map/ppermute | solution.py:22
  270.9 1.7 reshape.351
  272.6 2.9 multiply_reduce_fusion.1
  275.6 2.4 multiply_multiply_fusion
  278.1 3.2 collective-permute-done.1
  282.8 1.7 add_convert_fusion
  287.7 8.7 %collective-permute-done.2 = bf16[512,512]{1,0:T(8,128)(2,1)S(1)} collective-permute-done((bf16[512,512]{1,0:T(8,128)(2,1)}, bf16[512,512]{1,0:T(8,128)(2,1)S(1)}, u32[]{:S(2)}, u32[]{:S(2)}) %collective-permute-start.2) | collective-permute-done | bytes 524320 | tf_op jit(solution)/shard_map/ppermute | solution.py:144
  296.5 1.6 broadcast_select_fusion.1
  300.1 4.8 %fusion = (f32[2,2,512]{2,1,0:T(2,128)S(1)}, f32[2,1536,512,2]{2,1,3,0:T(8,128)S(1)}) fusion(pred[512,1536]{0,1:T(8,128)(4,1)} %get-tuple-element.37, bf16[1536,2,128,1]{0,2,3,1:T(8,128)(2,1)S(1)} %bitcast.127, bf16[512,2,2,128]{3,0,2,1:T(8,128)(2,1)} %bitcast.130), kind=kOutput, calls=%fused_computation.2 | convolution fusion | flops 814741504 | bytes 14688256 | tf_op jit(solution)/shard_map/qkgd,skd->kgqs/dot_general | solution.py:463
  304.9 3.4 divide_convert_fusion.1
  312.6 4.9 %fusion.2 = (f32[2,2,512]{2,1,0:T(2,128)S(1)}, f32[2,1536,512,2]{2,1,3,0:T(8,128)S(1)}) fusion(pred[512,1536]{0,1:T(8,128)(4,1)S(1)} %copy-done.14, bf16[1536,2,128,1]{0,2,3,1:T(8,128)(2,1)} %bitcast.126, bf16[512,2,2,128]{3,0,2,1:T(8,128)(2,1)S(1)} %bitcast.129), kind=kOutput, calls=%fused_computation.4 | convolution fusion | flops 814741504 | bytes 14688256 | tf_op jit(solution)/shard_map/qkgd,skd->kgqs/dot_general | solution.py:463
  317.6 2.8 divide_convert_fusion
  321.2 5.8 %convolution_convert_fusion = bf16[256,5376]{1,0:T(8,128)(2,1)} fusion(bf16[5376,512]{1,0:T(8,128)(2,1)} %bitcast.113, s32[]{:T(128)S(6)} %select_n.116, s32[]{:T(128)S(6)} %select_n.112, bf16[1,2,256,512]{3,2,1,0:T(8,128)(2,1)S(1)} %copy.66, bf16[1,2,256,512]{3,2,1,0:T(8,128)(2,1)S(1)} %copy.67), kind=kOutput, calls=%fused_computation.6 | convolution fusion | flops 1410793472 | bytes 9306120 | tf_op jit(solution)/shard_map/dot_general | solution.py:484
  327.0 5.8 %convolution_convert_fusion.1 = bf16[256,5376]{1,0:T(8,128)(2,1)} fusion(bf16[5376,512]{1,0:T(8,128)(2,1)} %bitcast.114, s32[]{:T(128)S(6)} %select_n.110, s32[]{:T(128)S(6)} %select_n.112, bf16[1,2,256,512]{3,2,1,0:T(8,128)(2,1)S(1)} %copy.66, bf16[1,2,256,512]{3,2,1,0:T(8,128)(2,1)S(1)} %copy.67), kind=kOutput, calls=%fused_computation.7 | convolution fusion | flops 1410793472 | bytes 9306120 | tf_op jit(solution)/shard_map/dot_general | solution.py:484
  333.4 5.2 %fusion.67 = (bf16[256,5376]{1,0:T(8,128)(2,1)S(1)}, f32[256,5376]{1,0:T(8,128)S(1)}) fusion(bf16[5376,512]{1,0:T(8,128)(2,1)} %bitcast.115, s32[]{:T(128)S(6)} %select_n.116, s32[]{:T(128)S(6)} %select_n.114, bf16[1,2,256,512]{3,2,1,0:T(8,128)(2,1)S(1)} %copy.66, bf16[1,2,256,512]{3,2,1,0:T(8,128)(2,1)S(1)} %copy.67, ...), kind=kOutput, calls=%fused_computation.113 | convolution fusion | flops 1413545984 | bytes 17563656 | tf_op jit(solution)/shard_map/dot_general | solution.py:484
  338.8 17.8 %collective-permute-start.6 = (bf16[128,5376]{1,0:T(8,128)(2,1)S(1)}, bf16[128,5376]{1,0:T(8,128)(2,1)S(1)}, u32[]{:S(2)}, u32[]{:S(2)}) collective-permute-start(bf16[128,5376]{1,0:T(8,128)(2,1)S(1)} %slice.98), channel_id=1, source_target_pairs={{0,8},{8,0},{16,24},{24,16},{1,9},{9,1},{17,25},{25,17},{2,10},{10... | collective-permute-start | bytes 4128776 | tf_op jit(solution)/shard_map/ppermute | solution.py:144
  356.6 3.4 convert_add_fusion.1
  361.6 12.6 %collective-permute-start.10 = (bf16[128,2688]{1,0:T(8,128)(2,1)S(1)}, bf16[128,2688]{1,0:T(8,128)(2,1)S(1)}, u32[]{:S(2)}, u32[]{:S(2)}) collective-permute-start(bf16[128,2688]{1,0:T(8,128)(2,1)S(1)} %fusion.20), channel_id=1, source_target_pairs={{0,8},{8,0},{16,24},{24,16},{1,9},{9,1},{17,25},{25,17},{2,10},{10... | collective-permute-start | bytes 2064392 | tf_op jit(solution)/shard_map/ppermute | solution.py:144
  374.2 13.4 %collective-permute-done.6 = bf16[128,5376]{1,0:T(8,128)(2,1)S(1)} collective-permute-done((bf16[128,5376]{1,0:T(8,128)(2,1)S(1)}, bf16[128,5376]{1,0:T(8,128)(2,1)S(1)}, u32[]{:S(2)}, u32[]{:S(2)}) %collective-permute-start.6) | collective-permute-done | bytes 1376288 | tf_op jit(solution)/shard_map/ppermute | solution.py:144
  389.3 12.1 %collective-permute-done.10 = bf16[128,2688]{1,0:T(8,128)(2,1)S(1)} collective-permute-done((bf16[128,2688]{1,0:T(8,128)(2,1)S(1)}, bf16[128,2688]{1,0:T(8,128)(2,1)S(1)}, u32[]{:S(2)}, u32[]{:S(2)}) %collective-permute-start.10) | collective-permute-done | bytes 688160 | tf_op jit(solution)/shard_map/ppermute | solution.py:144
  401.7 1.9 collective-permute-done.7
  405.4 2.2 collective-permute-done.11
  407.6 1.6 fusion.19
  (108 shorter events, 33.7 us)
Async XLA Ops:
  0.0 12.2 %copy-start.7 = (bf16[256,2688]{1,0:T(8,128)(2,1)S(1)}, bf16[256,2688]{1,0:T(8,128)(2,1)}, u32[]{:S(2)}) copy-start(bf16[256,2688]{1,0:T(8,128)(2,1)} %param.10) | copy-start | bytes 4128772
  0.0 12.1 %copy-start.19 = (f32[5376]{0:T(1024)S(1)}, f32[5376]{0:T(1024)}, u32[]{:S(2)}) copy-start(f32[5376]{0:T(1024)} %param.11) | copy-start | bytes 64516
  1.8 10.4 %collective-permute-start = (f32[256,1]{0,1:T(1,128)S(1)}, f32[256,1]{0,1:T(1,128)S(1)}, u32[]{:S(2)}, u32[]{:S(2)}) collective-permute-start(f32[256,1]{0,1:T(1,128)S(1)} %bitcast.134), channel_id=1, source_target_pairs={{0,1},{1,0},{2,3},{3,2},{4,5},{5,4},{6,7},{7,6},{8,9},{9,8},{10,11... | collective-permute-start | bytes 3080 | tf_op jit(solution)/shard_map/ppermute | solution.py:144
  12.6 3.4 copy-start.2
  248.3 1.8 copy-start.22
  248.8 3.7 copy-start.9
  256.8 3.9 copy-start.12
  256.8 3.8 copy-start.11
  256.8 14.1 %copy-start.1 = (f32[1024,512]{1,0:T(8,128)S(1)}, f32[1024,512]{1,0:T(8,128)}, u32[]{:S(2)}) copy-start(f32[1024,512]{1,0:T(8,128)} %copy-done) | copy-start | bytes 6291460
  259.7 28.0 %collective-permute-start.3 = (bf16[2,512,512]{2,1,0:T(8,128)(2,1)}, bf16[2,512,512]{2,1,0:T(8,128)(2,1)}, u32[]{:S(2)}, u32[]{:S(2)}) collective-permute-start(bf16[2,512,512]{2,1,0:T(8,128)(2,1)} %get-tuple-element.24), channel_id=1, source_target_pairs={{0,4},{4,0},{1,5},{5,1},{2,6},{6,2},{3,7},{7,3},{8,12},{12,8},{9,1... | collective-permute-start | bytes 3145736 | tf_op jit(solution)/shard_map/ppermute | solution.py:144
  261.6 19.7 %collective-permute-start.1 = (bf16[512,512]{1,0:T(8,128)(2,1)}, bf16[512,512]{1,0:T(8,128)(2,1)}, u32[]{:S(2)}, u32[]{:S(2)}) collective-permute-start(bf16[512,512]{1,0:T(8,128)(2,1)} %pad_maximum_fusion.6), channel_id=1, source_target_pairs={{0,16},{8,24},{1,17},{9,25},{2,18},{10,26},{3,19},{11,27},{4,20},{... | collective-permute-start | bytes 1572872 | tf_op jit(solution)/shard_map/ppermute | solution.py:22
  272.6 3.0 copy-start.6
  272.6 3.0 copy-start.21
  281.3 15.1 %collective-permute-start.2 = (bf16[512,512]{1,0:T(8,128)(2,1)}, bf16[512,512]{1,0:T(8,128)(2,1)S(1)}, u32[]{:S(2)}, u32[]{:S(2)}) collective-permute-start(bf16[512,512]{1,0:T(8,128)(2,1)} %collective-permute-done.1), channel_id=1, source_target_pairs={{0,4},{4,0},{1,5},{5,1},{2,6},{6,2},{3,7},{7,3},{8,12},{12,8},{9,1... | collective-permute-start | bytes 1572872 | tf_op jit(solution)/shard_map/ppermute | solution.py:144
  284.5 11.9 %copy-start.13 = (bf16[2,1,512,512]{3,2,1,0:T(8,128)(2,1)S(1)}, bf16[2,1,512,512]{3,2,1,0:T(8,128)(2,1)}, u32[]{:S(2)}) copy-start(bf16[2,1,512,512]{3,2,1,0:T(8,128)(2,1)} %get-tuple-element.23) | copy-start | bytes 3145732
  300.1 4.8 %copy-start.15 = (pred[512,1536]{0,1:T(8,128)(4,1)S(1)}, pred[512,1536]{0,1:T(8,128)(4,1)}, u32[]{:S(2)}) copy-start(pred[512,1536]{0,1:T(8,128)(4,1)} %get-tuple-element.37) | copy-start | bytes 2359300
  300.1 4.8 %copy-start.17 = (bf16[1536,256]{0,1:T(8,128)(2,1)S(1)}, bf16[1536,256]{0,1:T(8,128)(2,1)}, u32[]{:S(2)}) copy-start(bf16[1536,256]{0,1:T(8,128)(2,1)} %copy.54) | copy-start | bytes 2359300
  308.3 4.3 %copy-start.14 = (pred[512,1536]{0,1:T(8,128)(4,1)S(1)}, pred[512,1536]{0,1:T(8,128)(4,1)}, u32[]{:S(2)}) copy-start(pred[512,1536]{0,1:T(8,128)(4,1)} %get-tuple-element.38) | copy-start | bytes 2359300
  310.3 2.3 copy-start.18
  312.6 4.9 %copy-start.16 = (bf16[1536,256]{0,1:T(8,128)(2,1)S(1)}, bf16[1536,256]{0,1:T(8,128)(2,1)}, u32[]{:S(2)}) copy-start(bf16[1536,256]{0,1:T(8,128)(2,1)} %copy.61) | copy-start | bytes 2359300
  327.0 6.3 %collective-permute-start.5 = (bf16[256,5376]{1,0:T(8,128)(2,1)}, bf16[256,5376]{1,0:T(8,128)(2,1)}, u32[]{:S(2)}, u32[]{:S(2)}) collective-permute-start(bf16[256,5376]{1,0:T(8,128)(2,1)} %convolution_convert_fusion), channel_id=1, source_target_pairs={{0,2},{2,0},{1,3},{3,1},{4,6},{6,4},{5,7},{7,5},{8,10},{10,8},{9,1... | collective-permute-start | bytes 8257544 | tf_op jit(solution)/shard_map/ppermute | solution.py:144
  332.8 23.8 %collective-permute-start.4 = (bf16[256,5376]{1,0:T(8,128)(2,1)}, bf16[256,5376]{1,0:T(8,128)(2,1)}, u32[]{:S(2)}, u32[]{:S(2)}) collective-permute-start(bf16[256,5376]{1,0:T(8,128)(2,1)} %convolution_convert_fusion.1), channel_id=1, source_target_pairs={{0,2},{2,0},{1,3},{3,1},{4,6},{6,4},{5,7},{7,5},{8,10},{10,8},{9,1... | collective-permute-start | bytes 8257544 | tf_op jit(solution)/shard_map/ppermute | solution.py:144
  333.3 23.2 %slice-start = ((s8[5505024]{0:T(1024)(128)(4,1)}), s8[1310720]{0:T(1024)(128)(4,1)S(1)}, s32[]{:S(2)}) async-start(s8[5505024]{0:T(1024)(128)(4,1)} %bitcast.116), calls=%async_computation | async-start | bytes 2621440
  333.3 23.2 %slice-start.1 = ((s8[5505024]{0:T(1024)(128)(4,1)}), s8[4194304]{0:T(1024)(128)(4,1)S(1)}, s32[]{:S(2)}) async-start(s8[5505024]{0:T(1024)(128)(4,1)} %bitcast.116), calls=%async_computation.1 | async-start | bytes 8388608
  338.6 22.9 %collective-permute-start.9 = (bf16[128,2688]{1,0:T(8,128)(2,1)S(1)}, bf16[128,2688]{1,0:T(8,128)(2,1)S(1)}, u32[]{:S(2)}, u32[]{:S(2)}) collective-permute-start(bf16[128,2688]{1,0:T(8,128)(2,1)S(1)} %slice.104), channel_id=1, source_target_pairs={{0,1},{1,0},{2,3},{3,2},{4,5},{5,4},{6,7},{7,6},{8,9},{9,8},{10,11... | collective-permute-start | bytes 2064392 | tf_op jit(solution)/shard_map/ppermute | solution.py:144
  338.8 48.8 %collective-permute-start.6 = (bf16[128,5376]{1,0:T(8,128)(2,1)S(1)}, bf16[128,5376]{1,0:T(8,128)(2,1)S(1)}, u32[]{:S(2)}, u32[]{:S(2)}) collective-permute-start(bf16[128,5376]{1,0:T(8,128)(2,1)S(1)} %slice.98), channel_id=1, source_target_pairs={{0,8},{8,0},{16,24},{24,16},{1,9},{9,1},{17,25},{25,17},{2,10},{10... | collective-permute-start | bytes 4128776 | tf_op jit(solution)/shard_map/ppermute | solution.py:144
  360.1 29.2 %collective-permute-start.8 = (bf16[128,2688]{1,0:T(8,128)(2,1)S(1)}, bf16[128,2688]{1,0:T(8,128)(2,1)S(1)}, u32[]{:S(2)}, u32[]{:S(2)}) collective-permute-start(bf16[128,2688]{1,0:T(8,128)(2,1)S(1)} %slice.130), channel_id=1, source_target_pairs={{0,1},{1,0},{2,3},{3,2},{4,5},{5,4},{6,7},{7,6},{8,9},{9,8},{10,11... | collective-permute-start | bytes 2064392 | tf_op jit(solution)/shard_map/ppermute | solution.py:144
  361.6 39.8 %collective-permute-start.10 = (bf16[128,2688]{1,0:T(8,128)(2,1)S(1)}, bf16[128,2688]{1,0:T(8,128)(2,1)S(1)}, u32[]{:S(2)}, u32[]{:S(2)}) collective-permute-start(bf16[128,2688]{1,0:T(8,128)(2,1)S(1)} %fusion.20), channel_id=1, source_target_pairs={{0,8},{8,0},{16,24},{24,16},{1,9},{9,1},{17,25},{25,17},{2,10},{10... | collective-permute-start | bytes 2064392 | tf_op jit(solution)/shard_map/ppermute | solution.py:144
  387.9 15.6 %collective-permute-start.7 = (bf16[128,2688]{1,0:T(8,128)(2,1)S(1)}, bf16[128,2688]{1,0:T(8,128)(2,1)S(1)}, u32[]{:S(2)}, u32[]{:S(2)}) collective-permute-start(bf16[128,2688]{1,0:T(8,128)(2,1)S(1)} %slice.131), channel_id=1, source_target_pairs={{0,1},{1,0},{2,3},{3,2},{4,5},{5,4},{6,7},{7,6},{8,9},{9,8},{10,11... | collective-permute-start | bytes 2064392 | tf_op jit(solution)/shard_map/ppermute | solution.py:144
  401.6 3.7 copy-start.20
  401.6 6.0 %copy-start.8 = (bf16[256,2688]{1,0:T(8,128)(2,1)S(1)}, bf16[256,2688]{1,0:T(8,128)(2,1)}, u32[]{:S(2)}) copy-start(bf16[256,2688]{1,0:T(8,128)(2,1)} %param.10) | copy-start | bytes 4128772
  404.0 3.6 collective-permute-start.11
  (5 other events, 6.0 us)

commit v4 on v3

--- a/solution.py
+++ b/solution.py
@@ -282,7 +282,7 @@
 
     order = [1] + list(range(4, 6)) + list(range(2, 4)) + list(range(6, len(rels)))
     items = [(t, i) for t in range(4) for i in order]
-    window = len(order) + 1
+    window = len(order) - 2
 
     def start_item(n):
         if n < len(items):

time: 410 us -> 407 us (level)
  starting transfers between devices: 49.9 us -> 33.8 us
  Pallas kernels: 226 us -> 233 us
  waiting for transfers between devices: 41.5 us -> 48.2 us
    ppermute x11, starting transfers between devices: 40.6 us -> 24.2 us  [swap(): return lax.ppermute(block, axis, [(i, i ^ 1) for i in range(size)])]
    pallas_call x1, Pallas kernels: 226 us -> 233 us  [gathered_products(): pl.pallas_call(functools.partial(gather_kernel, planes), out_shape=(jax.S...]
    ppermute x11, waiting for transfers between devices: 38.3 us -> 43.6 us  [swap(): return lax.ppermute(block, axis, [(i, i ^ 1) for i in range(size)])]
  transfers between devices with their start and end apart: 12 -> 12, of which waited for: 6 -> 7; matrix products, arithmetic and copies ran while one was open for 9% -> 9% of each run, Pallas kernels for 0% -> 0%
where the time goes in v4:
time: 407 us; the launch traced here: 406 us
  Pallas kernels  233 us (57%)
  waiting for transfers between devices  48.2 us (12%)
  matrix products  36.1 us (9%)
  starting transfers between devices  33.8 us (8%)
  other arithmetic  32.1 us (8%)
  local copies, waits for them, and re-layouts  22.6 us (6%)
    pallas_call x1, Pallas kernels, gathered_products(): pl.pallas_call(functools.partial(gather_kernel, planes), out_shape=(jax.S...  233 us
    ppermute x11, waiting for transfers between devices, swap(): return lax.ppermute(block, axis, [(i, i ^ 1) for i in range(size)])  43.6 us
    ppermute x11, starting transfers between devices, swap(): return lax.ppermute(block, axis, [(i, i ^ 1) for i in range(size)])  24.2 us
    dot_general x4, matrix products, project(): lax.dot_general(block, o_all, (((1,), (1,)), ((), ())), preferred_element...  20.2 us
    dot_general x2, matrix products, attend(): jnp.einsum('qkgd,skd->kgqs', queries[i], window_keys, preferred_element_t...  9.69 us
    ppermute x1, starting transfers between devices, from_behind(): return lax.ppermute(block, axis, route)  9.59 us
  transfers between devices with their start and end apart: 12, of which 7 were waited for; matrix products, arithmetic and copies ran while one was open for 9% of the time, Pallas kernels for 0%

profile of v4, /device:TPU:0, one launch (start us, length us, event | category | flops | bytes accessed | tf_op | source)
XLA Modules:
  0.0 406.4 jit_solution(9793271503722702135)
XLA Ops:
  0.0 1.8 fusion.16
  1.8 3.0 collective-permute-start
  5.6 3.0 multiply_cosine_fusion
  9.4 2.7 fusion.14
  14.2 1.8 copy.50
  19.5 233.1 %shard_map.100 = (f32[1024,512]{1,0:T(8,128)S(1)}, f32[1024,512]{1,0:T(8,128)S(1)}, bf16[16,336,512]{2,1,0:T(8,128)(2,1)}) custom-call(bf16[8,256,336]{2,1,0:T(8,128)(2,1)S(1)} %bitcast.111, bf16[336,1024]{1,0:T(8,128)(2,1)S(1)} %copy-done.4, bf16[336,1024]{1,0:T(8,128)(2,1)S(1)} %copy-done.5, bf16[336,2048]{1,0:T(8,128)(2,1)S(1)} %copy-done.2, ...), custom_call_target="tpu_custom_call" | custom-call | tf_op jit(solution)/shard_map/pallas_call | solution.py:371
  256.8 2.4 multiply_multiply_fusion.1
  259.2 1.7 multiply_subtract_fusion
  263.5 2.8 fusion.64
  267.9 9.6 %collective-permute-start.1 = (bf16[512,512]{1,0:T(8,128)(2,1)}, bf16[512,512]{1,0:T(8,128)(2,1)}, u32[]{:S(2)}, u32[]{:S(2)}) collective-permute-start(bf16[512,512]{1,0:T(8,128)(2,1)} %pad_maximum_fusion.6), channel_id=1, source_target_pairs={{0,16},{8,24},{1,17},{9,25},{2,18},{10,26},{3,19},{11,27},{4,20},{... | collective-permute-start | bytes 1572872 | tf_op jit(solution)/shard_map/ppermute | solution.py:22
  277.5 1.7 reshape.351
  279.3 2.9 multiply_reduce_fusion.1
  282.3 2.4 multiply_multiply_fusion
  284.7 4.6 %collective-permute-done.1 = bf16[512,512]{1,0:T(8,128)(2,1)} collective-permute-done((bf16[512,512]{1,0:T(8,128)(2,1)}, bf16[512,512]{1,0:T(8,128)(2,1)}, u32[]{:S(2)}, u32[]{:S(2)}) %collective-permute-start.1) | collective-permute-done | bytes 524320 | tf_op jit(solution)/shard_map/ppermute | solution.py:22
  290.8 1.7 add_convert_fusion
  295.7 7.7 %collective-permute-done.2 = bf16[512,512]{1,0:T(8,128)(2,1)S(1)} collective-permute-done((bf16[512,512]{1,0:T(8,128)(2,1)}, bf16[512,512]{1,0:T(8,128)(2,1)S(1)}, u32[]{:S(2)}, u32[]{:S(2)}) %collective-permute-start.2) | collective-permute-done | bytes 524320 | tf_op jit(solution)/shard_map/ppermute | solution.py:144
  303.4 1.6 broadcast_select_fusion.1
  307.0 4.8 %fusion = (f32[2,2,512]{2,1,0:T(2,128)S(1)}, f32[2,1536,512,2]{2,1,3,0:T(8,128)S(1)}) fusion(pred[512,1536]{0,1:T(8,128)(4,1)} %get-tuple-element.37, bf16[1536,2,128,1]{0,2,3,1:T(8,128)(2,1)S(1)} %bitcast.127, bf16[512,2,2,128]{3,0,2,1:T(8,128)(2,1)} %bitcast.130), kind=kOutput, calls=%fused_computation.2 | convolution fusion | flops 814741504 | bytes 14688256 | tf_op jit(solution)/shard_map/qkgd,skd->kgqs/dot_general | solution.py:463
  311.8 3.4 divide_convert_fusion.1
  319.5 4.9 %fusion.2 = (f32[2,2,512]{2,1,0:T(2,128)S(1)}, f32[2,1536,512,2]{2,1,3,0:T(8,128)S(1)}) fusion(pred[512,1536]{0,1:T(8,128)(4,1)S(1)} %copy-done.14, bf16[1536,2,128,1]{0,2,3,1:T(8,128)(2,1)} %bitcast.126, bf16[512,2,2,128]{3,0,2,1:T(8,128)(2,1)S(1)} %bitcast.129), kind=kOutput, calls=%fused_computation.4 | convolution fusion | flops 814741504 | bytes 14688256 | tf_op jit(solution)/shard_map/qkgd,skd->kgqs/dot_general | solution.py:463
  324.5 2.8 divide_convert_fusion
  328.1 5.8 %convolution_convert_fusion = bf16[256,5376]{1,0:T(8,128)(2,1)} fusion(bf16[5376,512]{1,0:T(8,128)(2,1)} %bitcast.113, s32[]{:T(128)S(6)} %select_n.116, s32[]{:T(128)S(6)} %select_n.112, bf16[1,2,256,512]{3,2,1,0:T(8,128)(2,1)S(1)} %copy.66, bf16[1,2,256,512]{3,2,1,0:T(8,128)(2,1)S(1)} %copy.67), kind=kOutput, calls=%fused_computation.6 | convolution fusion | flops 1410793472 | bytes 9306120 | tf_op jit(solution)/shard_map/dot_general | solution.py:484
  333.9 5.8 %convolution_convert_fusion.1 = bf16[256,5376]{1,0:T(8,128)(2,1)} fusion(bf16[5376,512]{1,0:T(8,128)(2,1)} %bitcast.114, s32[]{:T(128)S(6)} %select_n.110, s32[]{:T(128)S(6)} %select_n.112, bf16[1,2,256,512]{3,2,1,0:T(8,128)(2,1)S(1)} %copy.66, bf16[1,2,256,512]{3,2,1,0:T(8,128)(2,1)S(1)} %copy.67), kind=kOutput, calls=%fused_computation.7 | convolution fusion | flops 1410793472 | bytes 9306120 | tf_op jit(solution)/shard_map/dot_general | solution.py:484
  340.3 5.2 %fusion.67 = (bf16[256,5376]{1,0:T(8,128)(2,1)S(1)}, f32[256,5376]{1,0:T(8,128)S(1)}) fusion(bf16[5376,512]{1,0:T(8,128)(2,1)} %bitcast.115, s32[]{:T(128)S(6)} %select_n.116, s32[]{:T(128)S(6)} %select_n.114, bf16[1,2,256,512]{3,2,1,0:T(8,128)(2,1)S(1)} %copy.66, bf16[1,2,256,512]{3,2,1,0:T(8,128)(2,1)S(1)} %copy.67, ...), kind=kOutput, calls=%fused_computation.113 | convolution fusion | flops 1413545984 | bytes 17563656 | tf_op jit(solution)/shard_map/dot_general | solution.py:484
  346.2 6.6 %collective-permute-start.6 = (bf16[128,5376]{1,0:T(8,128)(2,1)S(1)}, bf16[128,5376]{1,0:T(8,128)(2,1)S(1)}, u32[]{:S(2)}, u32[]{:S(2)}) collective-permute-start(bf16[128,5376]{1,0:T(8,128)(2,1)S(1)} %slice.98), channel_id=1, source_target_pairs={{0,8},{8,0},{16,24},{24,16},{1,9},{9,1},{17,25},{25,17},{2,10},{10... | collective-permute-start | bytes 4128776 | tf_op jit(solution)/shard_map/ppermute | solution.py:144
  352.8 3.4 convert_add_fusion.1
  357.9 5.9 %collective-permute-done.9 = bf16[128,2688]{1,0:T(8,128)(2,1)S(1)} collective-permute-done((bf16[128,2688]{1,0:T(8,128)(2,1)S(1)}, bf16[128,2688]{1,0:T(8,128)(2,1)S(1)}, u32[]{:S(2)}, u32[]{:S(2)}) %collective-permute-start.9) | collective-permute-done | bytes 688160 | tf_op jit(solution)/shard_map/ppermute | solution.py:144
  364.0 6.6 %collective-permute-start.10 = (bf16[128,2688]{1,0:T(8,128)(2,1)S(1)}, bf16[128,2688]{1,0:T(8,128)(2,1)S(1)}, u32[]{:S(2)}, u32[]{:S(2)}) collective-permute-start(bf16[128,2688]{1,0:T(8,128)(2,1)S(1)} %fusion.20), channel_id=1, source_target_pairs={{0,8},{8,0},{16,24},{24,16},{1,9},{9,1},{17,25},{25,17},{2,10},{10... | collective-permute-start | bytes 2064392 | tf_op jit(solution)/shard_map/ppermute | solution.py:144
  370.6 13.2 %collective-permute-done.6 = bf16[128,5376]{1,0:T(8,128)(2,1)S(1)} collective-permute-done((bf16[128,5376]{1,0:T(8,128)(2,1)S(1)}, bf16[128,5376]{1,0:T(8,128)(2,1)S(1)}, u32[]{:S(2)}, u32[]{:S(2)}) %collective-permute-start.6) | collective-permute-done | bytes 1376288 | tf_op jit(solution)/shard_map/ppermute | solution.py:144
  385.7 12.4 %collective-permute-done.10 = bf16[128,2688]{1,0:T(8,128)(2,1)S(1)} collective-permute-done((bf16[128,2688]{1,0:T(8,128)(2,1)S(1)}, bf16[128,2688]{1,0:T(8,128)(2,1)S(1)}, u32[]{:S(2)}, u32[]{:S(2)}) %collective-permute-start.10) | collective-permute-done | bytes 688160 | tf_op jit(solution)/shard_map/ppermute | solution.py:144
  398.4 2.4 collective-permute-done.7
  402.9 2.0 collective-permute-done.11
  (108 shorter events, 36.0 us)
Async XLA Ops:
  0.0 12.2 %copy-start.7 = (bf16[256,2688]{1,0:T(8,128)(2,1)S(1)}, bf16[256,2688]{1,0:T(8,128)(2,1)}, u32[]{:S(2)}) copy-start(bf16[256,2688]{1,0:T(8,128)(2,1)} %param.10) | copy-start | bytes 4128772
  0.0 12.1 %copy-start.19 = (f32[5376]{0:T(1024)S(1)}, f32[5376]{0:T(1024)}, u32[]{:S(2)}) copy-start(f32[5376]{0:T(1024)} %param.11) | copy-start | bytes 64516
  1.8 10.4 %collective-permute-start = (f32[256,1]{0,1:T(1,128)S(1)}, f32[256,1]{0,1:T(1,128)S(1)}, u32[]{:S(2)}, u32[]{:S(2)}) collective-permute-start(f32[256,1]{0,1:T(1,128)S(1)} %bitcast.134), channel_id=1, source_target_pairs={{0,1},{1,0},{2,3},{3,2},{4,5},{5,4},{6,7},{7,6},{8,9},{9,8},{10,11... | collective-permute-start | bytes 3080 | tf_op jit(solution)/shard_map/ppermute | solution.py:144
  12.6 3.4 copy-start.2
  255.0 1.8 copy-start.22
  255.5 3.7 copy-start.9
  263.5 3.6 copy-start.12
  263.5 3.5 copy-start.11
  263.5 14.0 %copy-start.1 = (f32[1024,512]{1,0:T(8,128)S(1)}, f32[1024,512]{1,0:T(8,128)}, u32[]{:S(2)}) copy-start(f32[1024,512]{1,0:T(8,128)} %copy-done) | copy-start | bytes 6291460
  266.4 29.3 %collective-permute-start.3 = (bf16[2,512,512]{2,1,0:T(8,128)(2,1)}, bf16[2,512,512]{2,1,0:T(8,128)(2,1)}, u32[]{:S(2)}, u32[]{:S(2)}) collective-permute-start(bf16[2,512,512]{2,1,0:T(8,128)(2,1)} %get-tuple-element.24), channel_id=1, source_target_pairs={{0,4},{4,0},{1,5},{5,1},{2,6},{6,2},{3,7},{7,3},{8,12},{12,8},{9,1... | collective-permute-start | bytes 3145736 | tf_op jit(solution)/shard_map/ppermute | solution.py:144
  267.9 21.4 %collective-permute-start.1 = (bf16[512,512]{1,0:T(8,128)(2,1)}, bf16[512,512]{1,0:T(8,128)(2,1)}, u32[]{:S(2)}, u32[]{:S(2)}) collective-permute-start(bf16[512,512]{1,0:T(8,128)(2,1)} %pad_maximum_fusion.6), channel_id=1, source_target_pairs={{0,16},{8,24},{1,17},{9,25},{2,18},{10,26},{3,19},{11,27},{4,20},{... | collective-permute-start | bytes 1572872 | tf_op jit(solution)/shard_map/ppermute | solution.py:22
  279.3 3.0 copy-start.6
  279.3 3.0 copy-start.21
  289.3 14.1 %collective-permute-start.2 = (bf16[512,512]{1,0:T(8,128)(2,1)}, bf16[512,512]{1,0:T(8,128)(2,1)S(1)}, u32[]{:S(2)}, u32[]{:S(2)}) collective-permute-start(bf16[512,512]{1,0:T(8,128)(2,1)} %collective-permute-done.1), channel_id=1, source_target_pairs={{0,4},{4,0},{1,5},{5,1},{2,6},{6,2},{3,7},{7,3},{8,12},{12,8},{9,1... | collective-permute-start | bytes 1572872 | tf_op jit(solution)/shard_map/ppermute | solution.py:144
  292.5 10.9 %copy-start.13 = (bf16[2,1,512,512]{3,2,1,0:T(8,128)(2,1)S(1)}, bf16[2,1,512,512]{3,2,1,0:T(8,128)(2,1)}, u32[]{:S(2)}) copy-start(bf16[2,1,512,512]{3,2,1,0:T(8,128)(2,1)} %get-tuple-element.23) | copy-start | bytes 3145732
  307.0 4.8 %copy-start.15 = (pred[512,1536]{0,1:T(8,128)(4,1)S(1)}, pred[512,1536]{0,1:T(8,128)(4,1)}, u32[]{:S(2)}) copy-start(pred[512,1536]{0,1:T(8,128)(4,1)} %get-tuple-element.37) | copy-start | bytes 2359300
  307.0 4.8 %copy-start.17 = (bf16[1536,256]{0,1:T(8,128)(2,1)S(1)}, bf16[1536,256]{0,1:T(8,128)(2,1)}, u32[]{:S(2)}) copy-start(bf16[1536,256]{0,1:T(8,128)(2,1)} %copy.54) | copy-start | bytes 2359300
  315.2 4.3 %copy-start.14 = (pred[512,1536]{0,1:T(8,128)(4,1)S(1)}, pred[512,1536]{0,1:T(8,128)(4,1)}, u32[]{:S(2)}) copy-start(pred[512,1536]{0,1:T(8,128)(4,1)} %get-tuple-element.38) | copy-start | bytes 2359300
  317.2 2.3 copy-start.18
  319.5 4.9 %copy-start.16 = (bf16[1536,256]{0,1:T(8,128)(2,1)S(1)}, bf16[1536,256]{0,1:T(8,128)(2,1)}, u32[]{:S(2)}) copy-start(bf16[1536,256]{0,1:T(8,128)(2,1)} %copy.61) | copy-start | bytes 2359300
  333.9 6.3 %collective-permute-start.5 = (bf16[256,5376]{1,0:T(8,128)(2,1)}, bf16[256,5376]{1,0:T(8,128)(2,1)}, u32[]{:S(2)}, u32[]{:S(2)}) collective-permute-start(bf16[256,5376]{1,0:T(8,128)(2,1)} %convolution_convert_fusion), channel_id=1, source_target_pairs={{0,2},{2,0},{1,3},{3,1},{4,6},{6,4},{5,7},{7,5},{8,10},{10,8},{9,1... | collective-permute-start | bytes 8257544 | tf_op jit(solution)/shard_map/ppermute | solution.py:144
  339.7 13.1 %collective-permute-start.4 = (bf16[256,5376]{1,0:T(8,128)(2,1)}, bf16[256,5376]{1,0:T(8,128)(2,1)}, u32[]{:S(2)}, u32[]{:S(2)}) collective-permute-start(bf16[256,5376]{1,0:T(8,128)(2,1)} %convolution_convert_fusion.1), channel_id=1, source_target_pairs={{0,2},{2,0},{1,3},{3,1},{4,6},{6,4},{5,7},{7,5},{8,10},{10,8},{9,1... | collective-permute-start | bytes 8257544 | tf_op jit(solution)/shard_map/ppermute | solution.py:144
  340.2 12.5 %slice-start = ((s8[5505024]{0:T(1024)(128)(4,1)}), s8[1310720]{0:T(1024)(128)(4,1)S(1)}, s32[]{:S(2)}) async-start(s8[5505024]{0:T(1024)(128)(4,1)} %bitcast.116), calls=%async_computation | async-start | bytes 2621440
  340.3 12.6 %slice-start.1 = ((s8[5505024]{0:T(1024)(128)(4,1)}), s8[4194304]{0:T(1024)(128)(4,1)S(1)}, s32[]{:S(2)}) async-start(s8[5505024]{0:T(1024)(128)(4,1)} %bitcast.116), calls=%async_computation.1 | async-start | bytes 8388608
  345.5 18.4 %collective-permute-start.9 = (bf16[128,2688]{1,0:T(8,128)(2,1)S(1)}, bf16[128,2688]{1,0:T(8,128)(2,1)S(1)}, u32[]{:S(2)}, u32[]{:S(2)}) collective-permute-start(bf16[128,2688]{1,0:T(8,128)(2,1)S(1)} %slice.104), channel_id=1, source_target_pairs={{0,1},{1,0},{2,3},{3,2},{4,5},{5,4},{6,7},{7,6},{8,9},{9,8},{10,11... | collective-permute-start | bytes 2064392 | tf_op jit(solution)/shard_map/ppermute | solution.py:144
  346.2 37.6 %collective-permute-start.6 = (bf16[128,5376]{1,0:T(8,128)(2,1)S(1)}, bf16[128,5376]{1,0:T(8,128)(2,1)S(1)}, u32[]{:S(2)}, u32[]{:S(2)}) collective-permute-start(bf16[128,5376]{1,0:T(8,128)(2,1)S(1)} %slice.98), channel_id=1, source_target_pairs={{0,8},{8,0},{16,24},{24,16},{1,9},{9,1},{17,25},{25,17},{2,10},{10... | collective-permute-start | bytes 4128776 | tf_op jit(solution)/shard_map/ppermute | solution.py:144
  356.3 29.3 %collective-permute-start.8 = (bf16[128,2688]{1,0:T(8,128)(2,1)S(1)}, bf16[128,2688]{1,0:T(8,128)(2,1)S(1)}, u32[]{:S(2)}, u32[]{:S(2)}) collective-permute-start(bf16[128,2688]{1,0:T(8,128)(2,1)S(1)} %slice.130), channel_id=1, source_target_pairs={{0,1},{1,0},{2,3},{3,2},{4,5},{5,4},{6,7},{7,6},{8,9},{9,8},{10,11... | collective-permute-start | bytes 2064392 | tf_op jit(solution)/shard_map/ppermute | solution.py:144
  364.0 34.1 %collective-permute-start.10 = (bf16[128,2688]{1,0:T(8,128)(2,1)S(1)}, bf16[128,2688]{1,0:T(8,128)(2,1)S(1)}, u32[]{:S(2)}, u32[]{:S(2)}) collective-permute-start(bf16[128,2688]{1,0:T(8,128)(2,1)S(1)} %fusion.20), channel_id=1, source_target_pairs={{0,8},{8,0},{16,24},{24,16},{1,9},{9,1},{17,25},{25,17},{2,10},{10... | collective-permute-start | bytes 2064392 | tf_op jit(solution)/shard_map/ppermute | solution.py:144
  384.1 16.7 %collective-permute-start.7 = (bf16[128,2688]{1,0:T(8,128)(2,1)S(1)}, bf16[128,2688]{1,0:T(8,128)(2,1)S(1)}, u32[]{:S(2)}, u32[]{:S(2)}) collective-permute-start(bf16[128,2688]{1,0:T(8,128)(2,1)S(1)} %slice.131), channel_id=1, source_target_pairs={{0,1},{1,0},{2,3},{3,2},{4,5},{5,4},{6,7},{7,6},{8,9},{9,8},{10,11... | collective-permute-start | bytes 2064392 | tf_op jit(solution)/shard_map/ppermute | solution.py:144
  398.3 4.5 %copy-start.20 = (f32[5376]{0:T(1024)S(1)}, f32[5376]{0:T(1024)}, u32[]{:S(2)}) copy-start(f32[5376]{0:T(1024)} %param.18) | copy-start | bytes 64516
  398.3 6.5 %copy-start.8 = (bf16[256,2688]{1,0:T(8,128)(2,1)S(1)}, bf16[256,2688]{1,0:T(8,128)(2,1)}, u32[]{:S(2)}) copy-start(bf16[256,2688]{1,0:T(8,128)(2,1)} %param.10) | copy-start | bytes 4128772
  401.2 3.6 collective-permute-start.11
  (5 other events, 6.0 us)
